TPU v7x, 256 devices: a whole 4x4x8 slice. The times are simulated.
256 devices in a mesh: rep: 8 (over x, z_hi), zero: 32 (over z_lo, y, core).
Axes of the slice: x: 4, y: 4, z: 8 (z_hi: 2, z_lo: 4; z = z_hi * 4 + z_lo), core: 2. Of those that a mesh axis runs over, the one named last changes fastest.
Arguments:
- gated_input: bfloat16 [8, 4096, 4096], P('rep', 'zero'), may hold values from -6 to 6
- query_gate: bfloat16 [8, 4096, 4096], P('rep', 'zero'), may hold values from -12 to 12
- cotangent: bfloat16 [8, 4096, 4096], P('rep', 'zero'), may hold values from -8 to 8
- filters: float32 [8, 256, 128], P('rep', 'zero'), may hold values from -0.5 to 0.5
- first_moment: float32 [8, 256, 128], P('rep', 'zero'), may hold values from -0.03125 to 0.03125
- second_moment: float32 [8, 256, 128], P('rep', 'zero'), may hold values from 1e-06 to 0.0001
- step_index: int32 [1], replicated, may hold values from 0 to 999
Outputs:
- query_grad: bfloat16 [8, 4096, 4096], P('rep', 'zero')
- input_grad: bfloat16 [8, 4096, 4096], P('rep', 'zero')
- new_filters: float32 [8, 256, 128], P('rep', 'zero')
All inputs are finite; a program needn't handle non-finite values.
Results may differ from a plain program's by a relative error of at most 0.007.
Values may be sent and summed in bfloat16 or wider, within the bound.
A program may use at most 256 MiB of HBM per device.

v0:
```python
from functools import partial

import jax
import jax.numpy as jnp
from jax import lax
from jax.sharding import PartitionSpec as P

CLIP_NORM = 1.0
BETA_ONE = 0.9
BETA_TWO = 0.95
LEARN_RATE = 0.05
ADAM_EPS = 1e-08


def swapped(value, axis, apart):
    mask = 2**apart
    pairs = [(source, source ^ mask) for source in range(lax.axis_size(axis))]
    return lax.ppermute(value, axis, pairs)


def passed_along(block, axis, distance):
    devices = range(lax.axis_size(axis))
    route = [(i - distance, i) for i in devices if i - distance in devices]
    return lax.ppermute(block, axis, route)


def circulant(half_filters):
    groups_all, filter_len = half_filters.shape
    flipped = half_filters[:, ::-1]
    doubled = jnp.concatenate([flipped, flipped], axis=1)
    tiled = jnp.tile(doubled, (1, filter_len))
    trimmed = tiled[:, : filter_len * (2 * filter_len - 1)]
    return trimmed.reshape(groups_all, filter_len, 2 * filter_len - 1)[:, :, filter_len - 1 :]


def blocked(rows_major, groups_all, filter_len):
    tok_rows, channels = rows_major.shape
    return rows_major.T.reshape(
        groups_all, channels // groups_all, tok_rows // filter_len, filter_len
    )


def unblocked(blocks):
    groups_all, group_width, block_count, filter_len = blocks.shape
    return blocks.reshape(groups_all * group_width, block_count * filter_len).T


def swap_bit(values, bit_number):
    return swapped(values, "rep", bit_number)


def on_device(gated_input, query_gate, cotangent, filters, first_moment, second_moment, step_index):
    inputs = gated_input[0]
    gate_values = query_gate[0]
    upstream = cotangent[0]
    tok_rows, channels = inputs.shape
    filter_len = filters.shape[2]
    half_filters = lax.all_gather(filters[0].astype(jnp.bfloat16), "zero", axis=0, tiled=True)
    groups_all = half_filters.shape[0]
    circ_table = circulant(half_filters)
    index_row = lax.broadcasted_iota(jnp.int32, (filter_len, filter_len), 0)
    index_col = lax.broadcasted_iota(jnp.int32, (filter_len, filter_len), 1)
    lower_mask = (index_row >= index_col)[None]
    zero_half = jnp.zeros((), jnp.bfloat16)
    table_cur = jnp.where(lower_mask, circ_table, zero_half)
    table_prev = jnp.where(lower_mask, zero_half, circ_table)
    upstream_wide = upstream.astype(jnp.float32)
    mixed_rows = (upstream_wide * gate_values.astype(jnp.float32)).astype(jnp.bfloat16)
    tail_rows = passed_along(inputs, "zero", 1)
    head_rows = passed_along(mixed_rows, "zero", -1)
    input_ext = jnp.concatenate([tail_rows, inputs], axis=0)
    mixed_ext = jnp.concatenate([mixed_rows, head_rows], axis=0)
    input_blocks = blocked(input_ext, groups_all, filter_len)
    mixed_blocks = blocked(mixed_ext, groups_all, filter_len)
    input_cur = input_blocks[:, :, 1:]
    input_prev = input_blocks[:, :, :-1]
    mixed_own = mixed_blocks[:, :, :-1]
    mixed_next = mixed_blocks[:, :, 1:]
    conv_out = jnp.einsum(
        "gik,gcbk->gcbi", table_cur, input_cur, preferred_element_type=jnp.float32
    )
    conv_out = conv_out + jnp.einsum(
        "gik,gcbk->gcbi", table_prev, input_prev, preferred_element_type=jnp.float32
    )
    query_grad = (upstream_wide * unblocked(conv_out)).astype(jnp.bfloat16)
    back_blocks = jnp.einsum(
        "gki,gcbk->gcbi", table_cur, mixed_own, preferred_element_type=jnp.float32
    )
    back_blocks = back_blocks + jnp.einsum(
        "gki,gcbk->gcbi", table_prev, mixed_next, preferred_element_type=jnp.float32
    )
    input_grad = unblocked(back_blocks).astype(jnp.bfloat16)
    lag_cur = jnp.einsum("gcbi,gcbk->gik", mixed_own, input_cur, preferred_element_type=jnp.float32)
    lag_prev = jnp.einsum(
        "gcbi,gcbk->gik", mixed_own, input_prev, preferred_element_type=jnp.float32
    )
    square = filter_len * filter_len
    front_part = jnp.pad(
        jnp.where(lower_mask, lag_cur, 0.0).reshape(groups_all, square), ((0, 0), (filter_len, 0))
    )
    rear_part = jnp.pad(
        jnp.where(lower_mask, 0.0, lag_prev).reshape(groups_all, square), ((0, 0), (0, filter_len))
    )
    skewed = (front_part + rear_part).reshape(groups_all, filter_len, filter_len + 1).sum(axis=1)
    local_grad = skewed[:, 1:][:, ::-1]
    grad_shard = lax.psum_scatter(
        local_grad.astype(jnp.bfloat16), "zero", scatter_dimension=0, tiled=True
    ).astype(jnp.float32)
    total_sq = lax.psum(jnp.sum(grad_shard * grad_shard), "zero")
    clip_scale = jnp.minimum(1.0, CLIP_NORM / (jnp.sqrt(total_sq) + 1e-06))
    clipped = grad_shard * clip_scale
    step_count = step_index[0].astype(jnp.float32) + 1.0
    moment_one = BETA_ONE * first_moment[0] + (1.0 - BETA_ONE) * clipped
    moment_two = BETA_TWO * second_moment[0] + (1.0 - BETA_TWO) * clipped * clipped
    corrected_one = moment_one / (1.0 - jnp.power(BETA_ONE, step_count))
    corrected_two = moment_two / (1.0 - jnp.power(BETA_TWO, step_count))
    stepped = filters[0] - LEARN_RATE * corrected_one / (jnp.sqrt(corrected_two) + ADAM_EPS)
    bit_count = lax.axis_size("rep").bit_length() - 1
    partner_bit = step_index[0] % bit_count
    branches = [partial(swap_bit, bit_number=number) for number in range(bit_count)]
    partner_values = lax.switch(partner_bit, branches, stepped)
    new_filters = 0.5 * (stepped + partner_values)
    return (query_grad[None], input_grad[None], new_filters[None])


def solution(mesh):
    return jax.shard_map(
        on_device,
        mesh=mesh,
        in_specs=(
            P("rep", "zero", None),
            P("rep", "zero", None),
            P("rep", "zero", None),
            P("rep", "zero", None),
            P("rep", "zero", None),
            P("rep", "zero", None),
            P(),
        ),
        out_specs=(P("rep", "zero", None), P("rep", "zero", None), P("rep", "zero", None)),
        check_vma=False,
    )
```

profile of v0, /device:TPU:1, one launch (start us, length us, event | category | flops | bytes accessed | tf_op | source)
XLA Modules:
  0.0 655.8 jit_solution(9882947588974306157)
XLA Ops:
  7.2 4.6 collective-permute-start.3
  12.5 43.4 %all_gather.3 = bf16[256,128]{1,0:T(8,128)(2,1)S(1)} all-gather(bf16[8,128]{1,0:T(8,128)(2,1)S(1)} %bitcast_convert_fusion), channel_id=1, replica_groups=mesh['rep'=8,'zero'=32] {'zero'}, dimensions={0}, use_global_device_ids=true | all-gather | bytes 67584 | tf_op jit(solution)/shard_map/all_gather | solution.py:58
  57.4 41.7 %copy.39 = bf16[32,8,128,256]{3,1,2,0:T(8,128)(2,1)S(1)} copy(bf16[32,8,128,256]{3,2,1,0:T(8,128)(2,1)S(1)} %bitcast.60) | data formatting | bytes 33554432
  99.1 6.6 %slice.29 = bf16[256,32640]{1,0:T(8,128)(2,1)} slice(bf16[256,32768]{1,0:T(8,128)(2,1)S(1)} %bitcast.61), slice={[0:256], [0:32640]} | slice | bytes 33423360 | tf_op jit(solution)/shard_map/slice | solution.py:32
  105.8 56.8 %reshape.87 = bf16[256,128,255]{2,1,0:T(8,128)(2,1)} reshape(bf16[256,32640]{1,0:T(8,128)(2,1)} %slice.29) | data formatting | bytes 33423360 | tf_op jit(solution)/shard_map/reshape | solution.py:33
  166.5 2.5 reshape.85
  169.0 3.0 fusion.28
  172.1 9.6 %fusion.1 = f32[256,16,128]{2,1,0:T(8,128)S(1)} fusion(pred[128,128]{1,0:T(8,128)(4,1)S(1)} %iota_compare_fusion, bf16[256,128,255]{2,1,0:T(8,128)(2,1)} %reshape.87, bf16[256,16,1,128]{3,2,1,0:T(2,128)(2,1)S(1)} %get-tuple-element.13), kind=kOutput, calls=%fused_computation.6 | convolution fusion | flops 138412032 | bytes 11550720 | tf_op jit(solution)/shard_map/gik,gcbk->gcbi/dot_general | solution.py:79
  181.7 11.7 %fusion.10 = f32[256,16,128]{2,1,0:T(8,128)} fusion(f32[256,16,128]{2,1,0:T(8,128)S(1)} %fusion.1, pred[128,128]{1,0:T(8,128)(4,1)S(1)} %iota_compare_fusion, bf16[256,128,255]{2,1,0:T(8,128)(2,1)} %reshape.87, bf16[256,16,1,128]{3,2,1,0:T(2,128)(2,1)S(1)} %get-tuple-element.12), kind=kOutput, calls=%fused_computation.20 | convolution fusion | flops 138936320 | bytes 13647872 | tf_op jit(solution)/shard_map/gik,gcbk->gcbi/dot_general | solution.py:82
  195.5 3.0 fusion.9
  202.6 12.1 %collective-permute-done.4 = bf16[128,4096]{1,0:T(8,128)(2,1)} collective-permute-done((bf16[128,4096]{1,0:T(8,128)(2,1)S(1)}, bf16[128,4096]{1,0:T(8,128)(2,1)}, u32[]{:S(2)}, u32[]{:S(2)}) %collective-permute-start.4) | collective-permute-done | bytes 1048608 | tf_op jit(solution)/shard_map/ppermute | solution.py:24
  221.1 3.8 fusion.27
  225.0 10.6 %fusion = f32[256,16,128]{2,1,0:T(8,128)} fusion(pred[128,128]{1,0:T(8,128)(4,1)S(1)} %iota_compare_fusion, bf16[256,128,255]{2,1,0:T(8,128)(2,1)} %reshape.87, bf16[256,16,1,128]{3,2,1,0:T(2,128)(2,1)S(1)} %get-tuple-element.11), kind=kOutput, calls=%fused_computation.5 | convolution fusion | flops 138412032 | bytes 11550720 | tf_op jit(solution)/shard_map/gki,gcbk->gcbi/dot_general | solution.py:86
  235.5 7.2 %convolution_select_fusion = f32[256,128,128]{2,1,0:T(8,128)} fusion(pred[128,128]{1,0:T(8,128)(4,1)S(1)} %iota_compare_fusion, bf16[256,16,1,128]{3,2,1,0:T(2,128)(2,1)S(1)} %copy-done.3, bf16[256,16,1,128]{3,2,1,0:T(2,128)(2,1)S(1)} %get-tuple-element.11), kind=kOutput, calls=%fused_computation.1 | convolution fusion | flops 138412032 | bytes 18890752 | tf_op jit(solution)/shard_map/gcbi,gcbk->gik/dot_general | solution.py:94
  242.7 7.1 %convolution_select_fusion.1 = f32[256,128,128]{2,1,0:T(8,128)} fusion(pred[128,128]{1,0:T(8,128)(4,1)S(1)} %iota_compare_fusion, bf16[256,16,1,128]{3,2,1,0:T(2,128)(2,1)S(1)} %copy-done.1, bf16[256,16,1,128]{3,2,1,0:T(2,128)(2,1)S(1)} %get-tuple-element.11), kind=kOutput, calls=%fused_computation.2 | convolution fusion | flops 138412032 | bytes 18890752 | tf_op jit(solution)/shard_map/gcbi,gcbk->gik/dot_general | solution.py:93
  249.8 17.8 %copy.34 = f32[256,128,128]{0,2,1:T(8,128)} copy(f32[256,128,128]{2,1,0:T(8,128)} %convolution_select_fusion) | data formatting | bytes 33554432 | tf_op jit(solution)/shard_map/reshape | solution.py:102
  267.5 17.7 %copy.33 = f32[256,128,128]{0,2,1:T(8,128)} copy(f32[256,128,128]{2,1,0:T(8,128)} %convolution_select_fusion.1) | data formatting | bytes 33554432 | tf_op jit(solution)/shard_map/reshape | solution.py:99
  285.3 18.0 %pad_add_fusion = f32[256,16512]{0,1:T(8,128)} fusion(f32[256,16384]{0,1:T(8,128)} %bitcast.58, f32[256,16384]{0,1:T(8,128)} %bitcast.59), kind=kLoop, calls=%fused_computation | loop fusion | flops 4227072 | bytes 50462720 | tf_op jit(solution)/shard_map/add | solution.py:104
  303.3 18.0 %reshape.95 = f32[256,128,129]{0,2,1:T(8,128)} reshape(f32[256,16512]{0,1:T(8,128)} %pad_add_fusion) | data formatting | bytes 33816576 | tf_op jit(solution)/shard_map/reshape | solution.py:104
  321.3 7.3 %reduce_sum.18 = bf16[256,129]{0,1:T(8,128)(2,1)S(1)} reduce(f32[256,128,129]{0,2,1:T(8,128)} %reshape.95, f32[]{:T(128)} %constant.14.clone.1), dimensions={1}, to_apply=%region_0.1 | reduce | flops 4194048 | bytes 16974340 | tf_op jit(solution)/shard_map/reduce_sum | solution.py:104
  329.7 9.8 %add_convert_fusion = bf16[256,16,128]{2,1,0:T(8,128)(2,1)S(1)} fusion(f32[256,16,128]{2,1,0:T(8,128)} %fusion, pred[128,128]{1,0:T(8,128)(4,1)S(1)} %iota_compare_fusion, bf16[256,128,255]{2,1,0:T(8,128)(2,1)} %reshape.87, bf16[256,16,1,128]{3,2,1,0:T(2,128)(2,1)S(1)} %copy-done.4), kind=kOutput, calls=%fused_computation.19 | convolution fusion | flops 139460608 | bytes 12599296 | tf_op jit(solution)/shard_map/gki,gcbk->gcbi/dot_general | solution.py:89
  339.5 229.8 %all-reduce.5.cloned.1.call-done = bf16[256,128]{1,0:T(8,128)(2,1)} async-done(((bf16[256,128]{1,0:T(8,128)(2,1)}), bf16[256,128]{1,0:T(8,128)(2,1)}) %all-reduce.5.cloned.1.call-update) | async-done | bytes 65552
  572.0 70.1 %psum.7 = f32[]{:T(128)} all-reduce(f32[]{:T(128)} %fusion.18), channel_id=1, replica_groups=mesh['rep'=8,'zero'=32] {'zero'}, use_global_device_ids=true, to_apply=%region_3.4 | all-reduce | flops 1 | bytes 8 | tf_op jit(solution)/shard_map/psum | solution.py:109
  643.5 4.2 conditional.1
  (45 shorter events, 27.2 us)
Async XLA Ops:
  7.2 562.2 %all-reduce.5.cloned.1.call-start = ((), (), s32[]{:S(2)}) async-start(), calls=%async_computation | async-start | bytes 131072
  7.2 155.4 %collective-permute-start.3 = (bf16[128,4096]{1,0:T(8,128)(2,1)}, bf16[128,4096]{1,0:T(8,128)(2,1)}, u32[]{:S(2)}, u32[]{:S(2)}) collective-permute-start(bf16[128,4096]{1,0:T(8,128)(2,1)} %bitcast.65), channel_id=1, source_target_pairs={{0,1},{1,2},{2,3},{3,4},{4,5},{5,6},{6,7},{7,8},{8,9},{9,10},{10,1... | collective-permute-start | bytes 3145736 | tf_op jit(solution)/shard_map/ppermute | solution.py:24
  105.8 56.8 %copy-start.5 = (bf16[1,128,4096]{2,1,0:T(8,128)(2,1)S(1)}, bf16[1,128,4096]{2,1,0:T(8,128)(2,1)}, u32[]{:S(2)}) copy-start(bf16[1,128,4096]{2,1,0:T(8,128)(2,1)} %param.10) | copy-start | bytes 3145732
  172.0 9.7 %copy-start = (bf16[256,16,1,128]{3,2,1,0:T(2,128)(2,1)}, bf16[256,16,1,128]{3,2,1,0:T(2,128)(2,1)S(1)}, u32[]{:S(2)}) copy-start(bf16[256,16,1,128]{3,2,1,0:T(2,128)(2,1)S(1)} %get-tuple-element.13) | copy-start | bytes 3145732
  172.0 9.7 %copy-start.2 = (bf16[256,16,1,128]{3,2,1,0:T(2,128)(2,1)}, bf16[256,16,1,128]{3,2,1,0:T(2,128)(2,1)S(1)}, u32[]{:S(2)}) copy-start(bf16[256,16,1,128]{3,2,1,0:T(2,128)(2,1)S(1)} %get-tuple-element.12) | copy-start | bytes 3145732
  195.5 5.9 copy-start.9
  198.5 16.2 %collective-permute-start.4 = (bf16[128,4096]{1,0:T(8,128)(2,1)S(1)}, bf16[128,4096]{1,0:T(8,128)(2,1)}, u32[]{:S(2)}, u32[]{:S(2)}) collective-permute-start(bf16[128,4096]{1,0:T(8,128)(2,1)S(1)} %get-tuple-element.14), channel_id=1, source_target_pairs={{1,0},{2,1},{3,2},{4,3},{5,4},{6,5},{7,6},{8,7},{9,8},{10,9},{11,1... | collective-permute-start | bytes 3145736 | tf_op jit(solution)/shard_map/ppermute | solution.py:24
  225.0 10.6 %copy-start.3 = (bf16[256,16,1,128]{3,2,1,0:T(2,128)(2,1)S(1)}, bf16[256,16,1,128]{3,2,1,0:T(2,128)(2,1)}, u32[]{:S(2)}) copy-start(bf16[256,16,1,128]{3,2,1,0:T(2,128)(2,1)} %copy-done.2) | copy-start | bytes 3145732
  235.5 7.2 %copy-start.1 = (bf16[256,16,1,128]{3,2,1,0:T(2,128)(2,1)S(1)}, bf16[256,16,1,128]{3,2,1,0:T(2,128)(2,1)}, u32[]{:S(2)}) copy-start(bf16[256,16,1,128]{3,2,1,0:T(2,128)(2,1)} %copy-done) | copy-start | bytes 3145732
  321.3 8.4 %copy-start.4 = (bf16[256,16,1,128]{3,2,1,0:T(2,128)(2,1)S(1)}, bf16[256,16,1,128]{3,2,1,0:T(2,128)(2,1)}, u32[]{:S(2)}) copy-start(bf16[256,16,1,128]{3,2,1,0:T(2,128)(2,1)} %get-tuple-element.10) | copy-start | bytes 3145732
  329.7 313.0 %copy-start.6 = (f32[1,8,128]{2,1,0:T(8,128)S(1)}, f32[1,8,128]{2,1,0:T(8,128)}, u32[]{:S(2)}) copy-start(f32[1,8,128]{2,1,0:T(8,128)} %param.13) | copy-start | bytes 12292
  329.7 313.0 %copy-start.7 = (f32[1,8,128]{2,1,0:T(8,128)S(1)}, f32[1,8,128]{2,1,0:T(8,128)}, u32[]{:S(2)}) copy-start(f32[1,8,128]{2,1,0:T(8,128)} %param.15) | copy-start | bytes 12292
  329.7 313.0 %copy-start.8 = (f32[1,8,128]{2,1,0:T(8,128)S(1)}, f32[1,8,128]{2,1,0:T(8,128)}, u32[]{:S(2)}) copy-start(f32[1,8,128]{2,1,0:T(8,128)} %param.14) | copy-start | bytes 12292
  643.5 4.2 collective-permute-start.2
Sparse Core Ops, SparseCore 0:
  329.8 239.4 all-reduce.4
where the time goes:
time: 659 us; the launch traced here: 656 us
  waiting for transfers between devices  244 us (37%)
  local copies, waits for them, and re-layouts  182 us (28%)
  blocking collectives  113 us (17%)
  matrix products  55.9 us (8%)
  other arithmetic  35.1 us (5%)
  between operations  16.4 us (2%)
  starting transfers between devices  9.23 us (1%)
    unnamed x2, waiting for transfers between devices  230 us
    psum x1, blocking collectives, on_device(): total_sq = lax.psum(jnp.sum(grad_shard * grad_shard), 'zero')  70.1 us
    reshape x1, local copies, waits for them, and re-layouts, circulant(): trimmed.reshape(groups_all, filter_len, 2 * filter_len - 1)  56.8 us
    all_gather x1, blocking collectives, on_device(): lax.all_gather(filters[0].astype(jnp.bfloat16), 'zero', axis=0, tiled=True)  43.4 us
    unnamed x22, local copies, waits for them, and re-layouts  42.4 us
    reshape x1, local copies, waits for them, and re-layouts, on_device(): (front_part + rear_part).reshape(groups_all, filter_len, filter_len + 1)  18 us
    add x1, other arithmetic, on_device(): front_part + rear_part  18 us
    reshape x1, local copies, waits for them, and re-layouts, on_device(): jnp.where(lower_mask, 0.0, lag_prev).reshape(groups_all, square)  17.8 us
  transfers between devices with their start and end apart: 4, of which 3 were waited for; matrix products, arithmetic and copies ran while one was open for 18% of the time, Pallas kernels for 0%

commit v1 on v0

v1 whole, which is shorter than its diff:
```python
import math

import jax
import jax.numpy as jnp
from jax import lax
from jax.experimental import pallas as pl
from jax.experimental.pallas import tpu as pltpu
from jax.sharding import PartitionSpec as P

CLIP_NORM = 1.0
BETA_ONE = 0.9
BETA_TWO = 0.95
LEARN_RATE = 0.05
ADAM_EPS = 1e-08

BF = jnp.bfloat16
F32 = jnp.float32
MESH = pl.DeviceIdType.MESH

ZERO = 32
CHUNKS = 8
TILES = 4
HALF = CHUNKS // 2
WIDE = TILES * 128
GROUPS = TILES * 8


def lane_ids():
    return lax.broadcasted_iota(jnp.int32, (16, 128), 1)


def row_ids():
    return lax.broadcasted_iota(jnp.int32, (16, 128), 0)


def exchange(blocks):
    part = lane_ids() // 16
    r = [blocks[0]] + [pltpu.roll(blocks[a], 16 * a, 1) for a in range(1, 8)]
    for s in (1, 2, 4):
        pick = (part & s) != 0
        r = [jnp.where(pick, r[(i + s) % 8], r[i]) for i in range(8)]
    return [r[0]] + [pltpu.roll(r[8 - g], 128 - 16 * g, 1) for g in range(1, 8)]


def windows(low, high):
    lanes = lane_ids()
    out = [low]
    for q in range(1, 8):
        out.append(pltpu.roll(jnp.where(lanes >= 16 * q, low, high), 128 - 16 * q, 1))
    return out + [high]


def forward_taps(row):
    taps = jnp.take_along_axis(
        jnp.broadcast_to(row, (16, 128)), (row_ids() - lane_ids()) & 127, axis=1
    )
    keep = lane_ids() > row_ids()
    none = jnp.zeros_like(taps)
    first, last = jnp.where(keep, taps, none), jnp.where(keep, none, taps)
    return jnp.concatenate([first, last[:, :16]], axis=1).astype(BF)


def backward_taps(row):
    taps = jnp.take_along_axis(
        jnp.broadcast_to(row, (16, 128)), (lane_ids() - row_ids()) & 127, axis=1
    )
    keep = lane_ids() >= row_ids()
    none = jnp.zeros_like(taps)
    first, last = jnp.where(keep, taps, none), jnp.where(keep, none, taps)
    return jnp.concatenate([first, last[:, :16]], axis=1).astype(BF)


def pair_convolved(taps_two, wins_two):
    taps = jnp.concatenate(taps_two, axis=0)
    wins = jnp.concatenate(
        [jnp.concatenate([u, v], axis=1) for u, v in zip(*wins_two)], axis=0
    )
    out = jnp.dot(taps, wins, preferred_element_type=F32)
    return [out[:16, :128].astype(BF), out[16:, 128:].astype(BF)]


def pair_lags(own_two, wins_two):
    none = jnp.zeros((16, 128), BF)
    rows = jnp.concatenate(
        [jnp.concatenate([own_two[0], none], 1), jnp.concatenate([none, own_two[1]], 1)], 0
    )
    wins = jnp.concatenate(
        [jnp.concatenate([u, v], axis=1) for u, v in zip(*wins_two)], axis=0
    )
    out = lax.dot_general(rows, wins, (((1,), (1,)), ((), ())), preferred_element_type=F32)
    return [out[:16], out[16:]]


def diagonal(lag, forward):
    tail = jnp.concatenate([lag[:, 128:144], jnp.zeros((16, 112), F32)], axis=1)
    if forward:
        keep, index = lane_ids() > row_ids(), (row_ids() - lane_ids()) & 127
    else:
        keep, index = lane_ids() >= row_ids(), (lane_ids() + row_ids()) & 127
    turned = jnp.take_along_axis(jnp.where(keep, lag[:, :128], tail), index, axis=1)
    return turned[:8] + turned[8:]


def kernel(
    x_hbm,
    gate_hbm,
    ct_hbm,
    filt_ref,
    one_ref,
    two_ref,
    step_ref,
    qg_hbm,
    ig_hbm,
    new_ref,
    x_in,
    gate_in,
    ct_in,
    x_own,
    m_own,
    x_prev,
    m_next,
    taps,
    grads,
    shares,
    squares,
    stepped,
    partners,
    qg,
    ig,
    x_ld,
    gate_ld,
    ct_ld,
    x_snd,
    x_rcv,
    m_snd,
    m_rcv,
    f_snd,
    f_rcv,
    g_snd,
    g_rcv,
    s_snd,
    s_rcv,
    p_snd,
    p_rcv,
    qg_st,
    ig_st,
):
    me = lax.axis_index("zero")
    rep = lax.axis_index("rep")
    has_next = me < ZERO - 1
    has_prev = me > 0
    mates = [
        rep + 1 - 2 * lax.rem(rep, 2),
        rep + 2 - 4 * lax.rem(lax.div(rep, 2), 2),
        lax.rem(rep + 4, 8),
    ]

    def ahead(d):
        return lax.rem(me + d, ZERO)

    def behind(d):
        return lax.rem(me + ZERO - d, ZERO)

    barrier = pltpu.get_barrier_semaphore()

    @pl.loop(1, ZERO)
    def _(d):
        pl.semaphore_signal(barrier, 1, device_id={"zero": ahead(d)}, device_id_type=MESH)

    for mate in mates:
        pl.semaphore_signal(barrier, 1, device_id={"rep": mate}, device_id_type=MESH)

    def wide(i):
        return pl.ds(pl.multiple_of(i * WIDE, WIDE), WIDE)

    def load(hbm, vmem, sem, i):
        return pltpu.make_async_copy(hbm.at[0, :, wide(i)], vmem.at[:, wide(i)], sem.at[i])

    @pl.loop(0, CHUNKS)
    def _(i):
        load(x_hbm, x_in, x_ld, i).start()
        load(ct_hbm, ct_in, ct_ld, CHUNKS - 1 - i).start()
        load(gate_hbm, gate_in, gate_ld, CHUNKS - 1 - i).start()

    @pl.when(me == 0)
    def _():
        x_prev[...] = jnp.zeros_like(x_prev)

    @pl.when(me == ZERO - 1)
    def _():
        m_next[...] = jnp.zeros_like(m_next)

    def slab(i):
        return pl.ds(i * GROUPS, GROUPS)

    def x_copy(i):
        return pltpu.make_async_remote_copy(
            src_ref=x_own.at[slab(i)],
            dst_ref=x_prev.at[slab(i)],
            send_sem=x_snd.at[i],
            recv_sem=x_rcv.at[i],
            device_id={"zero": ahead(1)},
            device_id_type=MESH,
        )

    def m_copy(i):
        return pltpu.make_async_remote_copy(
            src_ref=m_own.at[slab(i)],
            dst_ref=m_next.at[slab(i)],
            send_sem=m_snd.at[i],
            recv_sem=m_rcv.at[i],
            device_id={"zero": behind(1)},
            device_id_type=MESH,
        )

    def tile_of(t):
        return pl.ds(pl.multiple_of(t * 128, 128), 128)

    def arrange_x(i):
        load(x_hbm, x_in, x_ld, i).wait()
        for u in range(TILES):
            t = i * TILES + u
            out = exchange([x_in[16 * a : 16 * a + 16, tile_of(t)] for a in range(8)])
            for g in range(8):
                x_own[t * 8 + g] = out[g]

    def arrange_m(i):
        load(ct_hbm, ct_in, ct_ld, i).wait()
        load(gate_hbm, gate_in, gate_ld, i).wait()
        for u in range(TILES):
            t = i * TILES + u
            mixed = [
                (
                    ct_in[16 * a : 16 * a + 16, tile_of(t)].astype(F32)
                    * gate_in[16 * a : 16 * a + 16, tile_of(t)].astype(F32)
                ).astype(BF)
                for a in range(8)
            ]
            out = exchange(mixed)
            for g in range(8):
                m_own[t * 8 + g] = out[g]

    def send_x(i):
        @pl.when(has_next)
        def _():
            x_copy(i).start()

    def send_m(i):
        @pl.when(has_prev)
        def _():
            m_copy(i).start()

    def to_peer(src, dst, snd, rcv, d):
        return pltpu.make_async_remote_copy(
            src_ref=src,
            dst_ref=dst,
            send_sem=snd.at[d],
            recv_sem=rcv.at[d],
            device_id={"zero": ahead(d)},
            device_id_type=MESH,
        )

    arrange_x(0)
    pl.semaphore_wait(barrier, ZERO - 1 + len(mates))
    send_x(0)
    arrange_m(CHUNKS - 1)
    send_m(CHUNKS - 1)

    @pl.loop(1, ZERO)
    def _(d):
        to_peer(filt_ref.at[0], taps.at[me], f_snd, f_rcv, d).start()

    taps[me] = filt_ref[0]

    @pl.loop(1, CHUNKS)
    def _(i):
        arrange_x(i)
        send_x(i)
        arrange_m(CHUNKS - 1 - i)
        send_m(CHUNKS - 1 - i)

    @pl.loop(1, ZERO)
    def _(d):
        to_peer(filt_ref.at[0], taps.at[behind(d)], f_snd, f_rcv, d).wait_recv()

    def forward_tile(t, with_lag):
        conv, sums = [], []
        rows = taps[t]
        for g in range(0, 8, 2):
            n = t * 8 + g
            wins = [windows(x_prev[n + e], x_own[n + e]) for e in range(2)]
            conv += pair_convolved([forward_taps(rows[g + e : g + e + 1]) for e in range(2)], wins)
            if with_lag:
                sums += [diagonal(v, True) for v in pair_lags([m_own[n], m_own[n + 1]], wins)]
        if with_lag:
            grads[t] = jnp.sum(jnp.stack(sums), axis=1)
        out = exchange(conv)
        for a in range(8):
            at = (slice(16 * a, 16 * a + 16), tile_of(t))
            qg[at] = (ct_in[at].astype(F32) * out[a].astype(F32)).astype(BF)

    def backward_tile(t, with_lag):
        conv, sums = [], []
        rows = taps[t]
        for g in range(0, 8, 2):
            n = t * 8 + g
            wins = [windows(m_own[n + e], m_next[n + e]) for e in range(2)]
            conv += pair_convolved([backward_taps(rows[g + e : g + e + 1]) for e in range(2)], wins)
            if with_lag:
                sums += [diagonal(v, False) for v in pair_lags([x_own[n], x_own[n + 1]], wins)]
        if with_lag:
            grads[t] = jnp.sum(jnp.stack(sums), axis=1)
        out = exchange(conv)
        for a in range(8):
            ig[16 * a : 16 * a + 16, tile_of(t)] = out[a]

    def store(vmem, hbm, sem, i):
        return pltpu.make_async_copy(vmem.at[:, wide(i)], hbm.at[0, :, wide(i)], sem.at[i])

    def stage(i, with_lag):
        j = CHUNKS - 1 - i

        @pl.when(has_prev)
        def _():
            x_copy(i).wait_recv()

        @pl.when(has_next)
        def _():
            m_copy(j).wait_recv()

        @pl.loop(0, TILES)
        def _(u):
            forward_tile(i * TILES + u, with_lag)
            backward_tile(j * TILES + u, with_lag)

        store(qg, qg_hbm, qg_st, i).start()
        store(ig, ig_hbm, ig_st, j).start()

    @pl.loop(0, HALF)
    def _(i):
        stage(i, True)

    @pl.loop(1, ZERO)
    def _(d):
        to_peer(grads.at[ahead(d)], shares.at[d], g_snd, g_rcv, d).start()

    @pl.loop(HALF, HALF + 2)
    def _(i):
        stage(i, False)

    @pl.loop(1, ZERO)
    def _(d):
        to_peer(grads.at[ahead(d)], shares.at[d], g_snd, g_rcv, d).wait_recv()

    shares[0] = grads[me]
    grad = jnp.sum(shares[...], axis=0)
    squares[0] = grad * grad

    @pl.loop(1, ZERO)
    def _(d):
        to_peer(squares.at[0], squares.at[d], s_snd, s_rcv, d).start()

    stage(HALF + 2, False)

    @pl.loop(1, ZERO)
    def _(d):
        to_peer(squares.at[0], squares.at[d], s_snd, s_rcv, d).wait_recv()

    total = jnp.sum(jnp.sum(squares[...], axis=0), axis=(0, 1), keepdims=True)
    norm = jnp.sqrt(jnp.broadcast_to(total, (8, 128)))
    clipped = grad * jnp.minimum(1.0, CLIP_NORM / (norm + 1e-06))
    count = jnp.full((8, 128), step_ref[0], jnp.int32).astype(F32) + 1.0
    moment_one = BETA_ONE * one_ref[0] + (1.0 - BETA_ONE) * clipped
    moment_two = BETA_TWO * two_ref[0] + (1.0 - BETA_TWO) * clipped * clipped
    corrected_one = moment_one / (1.0 - jnp.exp(count * math.log(BETA_ONE)))
    corrected_two = moment_two / (1.0 - jnp.exp(count * math.log(BETA_TWO)))
    stepped[...] = filt_ref[0] - LEARN_RATE * corrected_one / (jnp.sqrt(corrected_two) + ADAM_EPS)

    def to_mate(b):
        return pltpu.make_async_remote_copy(
            src_ref=stepped,
            dst_ref=partners.at[b],
            send_sem=p_snd.at[b],
            recv_sem=p_rcv.at[b],
            device_id={"rep": mates[b]},
            device_id_type=MESH,
        )

    for b in range(3):
        to_mate(b).start()

    stage(HALF + 3, False)

    for b in range(3):
        to_mate(b).wait_recv()
    bit = lax.rem(jnp.full((8, 128), step_ref[0], jnp.int32), 3)
    partner = jnp.where(bit == 0, partners[0], jnp.where(bit == 1, partners[1], partners[2]))
    new_ref[0] = 0.5 * (stepped[...] + partner)

    for b in range(3):
        to_mate(b).wait_send()

    @pl.loop(1, ZERO)
    def _(d):
        to_peer(filt_ref.at[0], taps.at[me], f_snd, f_rcv, d).wait_send()
        to_peer(grads.at[ahead(d)], shares.at[d], g_snd, g_rcv, d).wait_send()
        to_peer(squares.at[0], squares.at[d], s_snd, s_rcv, d).wait_send()

    @pl.loop(0, CHUNKS)
    def _(i):
        store(qg, qg_hbm, qg_st, i).wait()
        store(ig, ig_hbm, ig_st, i).wait()

        @pl.when(has_next)
        def _():
            x_copy(i).wait_send()

        @pl.when(has_prev)
        def _():
            m_copy(i).wait_send()


def on_device(gated_input, query_gate, cotangent, filters, first_moment, second_moment, step_index):
    anywhere = pl.BlockSpec(memory_space=pl.ANY)
    vmem = pl.BlockSpec(memory_space=pltpu.VMEM)
    dma = pltpu.SemaphoreType.DMA
    _, rows, channels = gated_input.shape
    groups = channels // 16
    natural = pltpu.VMEM((rows, channels), BF)
    grouped = pltpu.VMEM((groups, 16, 128), BF)
    shards = pltpu.VMEM((ZERO, 8, 128), F32)
    return pl.pallas_call(
        kernel,
        name="hyena_step",
        out_shape=[
            jax.ShapeDtypeStruct(gated_input.shape, BF),
            jax.ShapeDtypeStruct(gated_input.shape, BF),
            jax.ShapeDtypeStruct(filters.shape, F32),
        ],
        in_specs=[anywhere] * 3 + [vmem] * 3 + [pl.BlockSpec(memory_space=pltpu.SMEM)],
        out_specs=[anywhere] * 2 + [vmem],
        scratch_shapes=[natural] * 3
        + [grouped] * 4
        + [shards] * 4
        + [pltpu.VMEM((8, 128), F32), pltpu.VMEM((3, 8, 128), F32)]
        + [natural] * 2
        + [dma((CHUNKS,))] * 7
        + [dma((ZERO,))] * 6
        + [dma((3,))] * 2
        + [dma((CHUNKS,))] * 2,
        compiler_params=pltpu.CompilerParams(
            collective_id=0, has_side_effects=True, vmem_limit_bytes=40 << 20
        ),
        cost_estimate=pl.CostEstimate(flops=4 << 30, bytes_accessed=8 << 20, transcendentals=0),
    )(gated_input, query_gate, cotangent, filters, first_moment, second_moment, step_index)


def solution(mesh):
    split = P("rep", "zero", None)
    return jax.shard_map(
        on_device,
        mesh=mesh,
        in_specs=(split,) * 6 + (P(),),
        out_specs=(split,) * 3,
        check_vma=False,
    )
```

time: 659 us -> 54.6 us (0.08)
  waiting for transfers between devices: 244 us -> 0 us
  local copies, waits for them, and re-layouts: 182 us -> 8.26 us
  blocking collectives: 113 us -> 0 us
  matrix products: 55.9 us -> 0 us
  Pallas kernels: 0 us -> 44.7 us
  other arithmetic: 35.1 us -> 0 us
  between operations: 16.4 us -> 1.3 us
  starting transfers between devices: 9.23 us -> 0 us
    unnamed x2 -> x0, waiting for transfers between devices: 230 us -> none
    reshape x7 -> x0, local copies, waits for them, and re-layouts: 118 us -> none  [the longest x1 56.8 us: circulant(): trimmed.reshape(groups_all, filter_len, 2 * filter_len - 1)]
    psum x1 -> x0, blocking collectives: 70.1 us -> none  [on_device(): total_sq = lax.psum(jnp.sum(grad_shard * grad_shard), 'zero')]
    dot_general x6 -> x0, matrix products: 55.9 us -> none  [the longest x1 11.7 us: on_device(): jnp.einsum('gik,gcbk->gcbi', table_prev, input_prev, preferred_element_ty...]
    pallas_call x0 -> x1, Pallas kernels: none -> 44.7 us  [on_device(): pl.pallas_call(kernel, name='hyena_step', out_shape=[jax.ShapeDtypeStruct...]
    all_gather x1 -> x0, blocking collectives: 43.4 us -> none  [on_device(): lax.all_gather(filters[0].astype(jnp.bfloat16), 'zero', axis=0, tiled=True)]
    unnamed x22 -> x15, local copies, waits for them, and re-layouts: 42.4 us -> 8.26 us
    add x1 -> x0, other arithmetic: 18 us -> none  [on_device(): front_part + rear_part]
  transfers between devices with their start and end apart: 4 -> 0, of which waited for: 3 -> 0; matrix products, arithmetic and copies ran while one was open for 18% -> 0% of each run, Pallas kernels for 0% -> 0%
where the time goes in v1:
time: 54.6 us; the launch traced here: 54.3 us
  Pallas kernels  44.7 us (82%)
  local copies, waits for them, and re-layouts  8.26 us (15%)
  between operations  1.3 us (2%)
    pallas_call x1, Pallas kernels, on_device(): pl.pallas_call(kernel, name='hyena_step', out_shape=[jax.ShapeDtypeStruct...  44.7 us
    unnamed x15, local copies, waits for them, and re-layouts  8.26 us

profile of v1, /device:TPU:1, one launch (start us, length us, event | category | flops | bytes accessed | tf_op | source)
XLA Modules:
  0.0 54.3 jit_solution(17299025984922051301)
XLA Ops:
  1.3 0.0 copy-start
  1.3 1.2 %copy-done = bf16[1,128,4096]{2,1,0:T(8,128)(2,1)S(1)} copy-done((bf16[1,128,4096]{2,1,0:T(8,128)(2,1)S(1)}, bf16[1,128,4096]{2,1,0:T(8,128)(2,1)}, u32[]{:S(2)}) %copy-start) | copy-done | bytes 1048600
  2.5 0.0 copy-start.1
  2.5 1.2 %copy-done.1 = bf16[1,128,4096]{2,1,0:T(8,128)(2,1)S(1)} copy-done((bf16[1,128,4096]{2,1,0:T(8,128)(2,1)S(1)}, bf16[1,128,4096]{2,1,0:T(8,128)(2,1)}, u32[]{:S(2)}) %copy-start.1) | copy-done | bytes 1048600
  3.7 0.0 copy-start.2
  3.7 1.2 %copy-done.2 = bf16[1,128,4096]{2,1,0:T(8,128)(2,1)S(1)} copy-done((bf16[1,128,4096]{2,1,0:T(8,128)(2,1)S(1)}, bf16[1,128,4096]{2,1,0:T(8,128)(2,1)}, u32[]{:S(2)}) %copy-start.2) | copy-done | bytes 1048600
  5.0 0.0 copy-start.3
  5.0 0.7 %copy-done.3 = f32[1,8,128]{2,1,0:T(8,128)S(1)} copy-done((f32[1,8,128]{2,1,0:T(8,128)S(1)}, f32[1,8,128]{2,1,0:T(8,128)}, u32[]{:S(2)}) %copy-start.3) | copy-done | bytes 4120
  5.6 0.0 copy-start.4
  5.6 0.7 %copy-done.4 = f32[1,8,128]{2,1,0:T(8,128)S(1)} copy-done((f32[1,8,128]{2,1,0:T(8,128)S(1)}, f32[1,8,128]{2,1,0:T(8,128)}, u32[]{:S(2)}) %copy-start.4) | copy-done | bytes 4120
  6.3 0.0 copy-start.5
  6.3 0.7 %copy-done.5 = f32[1,8,128]{2,1,0:T(8,128)S(1)} copy-done((f32[1,8,128]{2,1,0:T(8,128)S(1)}, f32[1,8,128]{2,1,0:T(8,128)}, u32[]{:S(2)}) %copy-start.5) | copy-done | bytes 4120
  7.0 44.7 %hyena_step.1 = (bf16[1,128,4096]{2,1,0:T(8,128)(2,1)S(1)}, bf16[1,128,4096]{2,1,0:T(8,128)(2,1)S(1)}, f32[1,8,128]{2,1,0:T(8,128)S(1)}) custom-call(bf16[1,128,4096]{2,1,0:T(8,128)(2,1)S(1)} %copy-done, bf16[1,128,4096]{2,1,0:T(8,128)(2,1)S(1)} %copy-done.1, bf16[1,128,4096]{2,1,0:T(8,128)(2,1)S(1)} %copy-done.2, f32[1,8,128]{2,1,0:T(8,128)S(1)} %copy-done.3, ...), custom_call_target="tpu_custom_call" | custom-call | flops 4294967296 | bytes 8388608 | tf_op jit(solution)/shard_map/hyena_step/pallas_call | solution.py:432
  51.7 1.0 %copy.14 = bf16[1,128,4096]{2,1,0:T(8,128)(2,1)} copy(bf16[1,128,4096]{2,1,0:T(8,128)(2,1)S(1)} %get-tuple-element.6) | data formatting | bytes 2097152
  52.7 1.0 %copy.15 = bf16[1,128,4096]{2,1,0:T(8,128)(2,1)} copy(bf16[1,128,4096]{2,1,0:T(8,128)(2,1)S(1)} %get-tuple-element.7) | data formatting | bytes 2097152
  53.7 0.6 %copy.16 = f32[1,8,128]{2,1,0:T(8,128)} copy(f32[1,8,128]{2,1,0:T(8,128)S(1)} %get-tuple-element.8) | data formatting | bytes 8192
Async XLA Ops:
  1.3 1.2 %copy-start = (bf16[1,128,4096]{2,1,0:T(8,128)(2,1)S(1)}, bf16[1,128,4096]{2,1,0:T(8,128)(2,1)}, u32[]{:S(2)}) copy-start(bf16[1,128,4096]{2,1,0:T(8,128)(2,1)} %x_hbm.1) | copy-start | bytes 3145732
  2.5 1.2 %copy-start.1 = (bf16[1,128,4096]{2,1,0:T(8,128)(2,1)S(1)}, bf16[1,128,4096]{2,1,0:T(8,128)(2,1)}, u32[]{:S(2)}) copy-start(bf16[1,128,4096]{2,1,0:T(8,128)(2,1)} %gate_hbm.1) | copy-start | bytes 3145732
  3.7 1.2 %copy-start.2 = (bf16[1,128,4096]{2,1,0:T(8,128)(2,1)S(1)}, bf16[1,128,4096]{2,1,0:T(8,128)(2,1)}, u32[]{:S(2)}) copy-start(bf16[1,128,4096]{2,1,0:T(8,128)(2,1)} %ct_hbm.1) | copy-start | bytes 3145732
  5.0 0.7 %copy-start.3 = (f32[1,8,128]{2,1,0:T(8,128)S(1)}, f32[1,8,128]{2,1,0:T(8,128)}, u32[]{:S(2)}) copy-start(f32[1,8,128]{2,1,0:T(8,128)} %filt_ref.1) | copy-start | bytes 12292
  5.6 0.7 %copy-start.4 = (f32[1,8,128]{2,1,0:T(8,128)S(1)}, f32[1,8,128]{2,1,0:T(8,128)}, u32[]{:S(2)}) copy-start(f32[1,8,128]{2,1,0:T(8,128)} %one_ref.1) | copy-start | bytes 12292
  6.3 0.7 %copy-start.5 = (f32[1,8,128]{2,1,0:T(8,128)S(1)}, f32[1,8,128]{2,1,0:T(8,128)}, u32[]{:S(2)}) copy-start(f32[1,8,128]{2,1,0:T(8,128)} %two_ref.1) | copy-start | bytes 12292

commit v2 on v1

v2 whole, which is shorter than its diff:
```python
import math

import jax
import jax.numpy as jnp
from jax import lax
from jax.experimental import pallas as pl
from jax.experimental.pallas import tpu as pltpu
from jax.sharding import PartitionSpec as P

CLIP_NORM = 1.0
BETA_ONE = 0.9
BETA_TWO = 0.95
LEARN_RATE = 0.05
ADAM_EPS = 1e-08

BF = jnp.bfloat16
F32 = jnp.float32
MESH = pl.DeviceIdType.MESH

ZERO = 32
CHUNKS = 16
TILES = 2
HALF = CHUNKS // 2
WIDE = TILES * 128
GROUPS = TILES * 8
EARLY = 8
RS_BESIDE = 5
NORM_BESIDE = 11


def lane_ids():
    return lax.broadcasted_iota(jnp.int32, (16, 128), 1)


def row_ids():
    return lax.broadcasted_iota(jnp.int32, (16, 128), 0)


def exchange(blocks):
    part = lane_ids() // 16
    r = [blocks[0]] + [pltpu.roll(blocks[a], 16 * a, 1) for a in range(1, 8)]
    for s in (1, 2, 4):
        pick = (part & s) != 0
        r = [jnp.where(pick, r[(i + s) % 8], r[i]) for i in range(8)]
    return [r[0]] + [pltpu.roll(r[8 - g], 128 - 16 * g, 1) for g in range(1, 8)]


def windows(low, high):
    lanes = lane_ids()
    out = [low]
    for q in range(1, 8):
        out.append(pltpu.roll(jnp.where(lanes >= 16 * q, low, high), 128 - 16 * q, 1))
    return out + [high]


def forward_taps(row):
    taps = jnp.take_along_axis(
        jnp.broadcast_to(row, (16, 128)), (row_ids() - lane_ids()) & 127, axis=1
    )
    keep = lane_ids() > row_ids()
    none = jnp.zeros_like(taps)
    first, last = jnp.where(keep, taps, none), jnp.where(keep, none, taps)
    return jnp.concatenate([first, last[:, :16]], axis=1).astype(BF)


def backward_taps(row):
    taps = jnp.take_along_axis(
        jnp.broadcast_to(row, (16, 128)), (lane_ids() - row_ids()) & 127, axis=1
    )
    keep = lane_ids() >= row_ids()
    none = jnp.zeros_like(taps)
    first, last = jnp.where(keep, taps, none), jnp.where(keep, none, taps)
    return jnp.concatenate([first, last[:, :16]], axis=1).astype(BF)


def pair_convolved(taps_two, wins_two):
    taps = jnp.concatenate(taps_two, axis=0)
    wins = jnp.concatenate(
        [jnp.concatenate([u, v], axis=1) for u, v in zip(*wins_two)], axis=0
    )
    out = jnp.dot(taps, wins, preferred_element_type=F32)
    return [out[:16, :128].astype(BF), out[16:, 128:].astype(BF)]


def pair_lags(own_two, wins_two):
    none = jnp.zeros((16, 128), BF)
    rows = jnp.concatenate(
        [jnp.concatenate([own_two[0], none], 1), jnp.concatenate([none, own_two[1]], 1)], 0
    )
    wins = jnp.concatenate(
        [jnp.concatenate([u, v], axis=1) for u, v in zip(*wins_two)], axis=0
    )
    out = lax.dot_general(rows, wins, (((1,), (1,)), ((), ())), preferred_element_type=F32)
    return [out[:16], out[16:]]


def diagonal(lag, forward):
    tail = jnp.concatenate([lag[:, 128:144], jnp.zeros((16, 112), F32)], axis=1)
    if forward:
        keep, index = lane_ids() > row_ids(), (row_ids() - lane_ids()) & 127
    else:
        keep, index = lane_ids() >= row_ids(), (lane_ids() + row_ids()) & 127
    turned = jnp.take_along_axis(jnp.where(keep, lag[:, :128], tail), index, axis=1)
    return turned[:8] + turned[8:]


def kernel(
    x_hbm,
    gate_hbm,
    ct_hbm,
    filt_hbm,
    one_hbm,
    two_hbm,
    step_ref,
    qg_hbm,
    ig_hbm,
    new_hbm,
    x_in,
    gate_in,
    ct_in,
    x_own,
    m_own,
    x_prev,
    m_next,
    qg,
    ig,
    taps,
    grads,
    shares,
    squares,
    small,
    partners,
    x_ld,
    gate_ld,
    ct_ld,
    x_snd,
    x_rcv,
    m_snd,
    m_rcv,
    qg_st,
    ig_st,
    small_sem,
    p_snd,
    p_rcv,
    peer_sem,
):
    me = lax.axis_index("zero")
    rep = lax.axis_index("rep")
    has_next = me < ZERO - 1
    has_prev = me > 0
    mates = [
        rep + 1 - 2 * lax.rem(rep, 2),
        rep + 2 - 4 * lax.rem(lax.div(rep, 2), 2),
        lax.rem(rep + 4, 8),
    ]
    filt, one, two, stepped, sibling, renewed = (small.at[i] for i in range(6))
    core = lax.rem(me, 2)
    chip = lax.div(me, 2)

    def ahead(d):
        return lax.rem(me + d, ZERO)

    barrier = pltpu.get_barrier_semaphore()

    @pl.loop(1, ZERO)
    def _(d):
        pl.semaphore_signal(barrier, 1, device_id={"zero": ahead(d)}, device_id_type=MESH)

    for mate in mates:
        pl.semaphore_signal(barrier, 1, device_id={"rep": mate}, device_id_type=MESH)

    def wide(i):
        return pl.ds(pl.multiple_of(i * WIDE, WIDE), WIDE)

    def load(hbm, vmem, sem, i):
        return pltpu.make_async_copy(hbm.at[0, :, wide(i)], vmem.at[:, wide(i)], sem.at[i])

    def load_small(hbm, i):
        return pltpu.make_async_copy(hbm.at[0], small.at[i], small_sem.at[i])

    for i, hbm in enumerate((filt_hbm, one_hbm, two_hbm)):
        load_small(hbm, i).start()

    @pl.loop(0, CHUNKS)
    def _(i):
        load(x_hbm, x_in, x_ld, i).start()
        load(ct_hbm, ct_in, ct_ld, CHUNKS - 1 - i).start()
        load(gate_hbm, gate_in, gate_ld, CHUNKS - 1 - i).start()

    @pl.when(me == 0)
    def _():
        x_prev[...] = jnp.zeros_like(x_prev)

    @pl.when(me == ZERO - 1)
    def _():
        m_next[...] = jnp.zeros_like(m_next)

    def slab(i):
        return pl.ds(i * GROUPS, GROUPS)

    def x_copy(i):
        return pltpu.make_async_remote_copy(
            src_ref=x_own.at[slab(i)],
            dst_ref=x_prev.at[slab(i)],
            send_sem=x_snd.at[i],
            recv_sem=x_rcv.at[i],
            device_id={"zero": ahead(1)},
            device_id_type=MESH,
        )

    def m_copy(i):
        return pltpu.make_async_remote_copy(
            src_ref=m_own.at[slab(i)],
            dst_ref=m_next.at[slab(i)],
            send_sem=m_snd.at[i],
            recv_sem=m_rcv.at[i],
            device_id={"zero": ahead(ZERO - 1)},
            device_id_type=MESH,
        )

    def tile_of(t):
        return pl.ds(pl.multiple_of(t * 128, 128), 128)

    def arrange(i, j):
        load(x_hbm, x_in, x_ld, i).wait()
        load(ct_hbm, ct_in, ct_ld, j).wait()
        load(gate_hbm, gate_in, gate_ld, j).wait()
        for u in range(TILES):
            t = i * TILES + u
            out = exchange([x_in[16 * a : 16 * a + 16, tile_of(t)] for a in range(8)])
            for g in range(8):
                x_own[t * 8 + g] = out[g]
            t = j * TILES + u
            mixed = [
                (
                    ct_in[16 * a : 16 * a + 16, tile_of(t)].astype(F32)
                    * gate_in[16 * a : 16 * a + 16, tile_of(t)].astype(F32)
                ).astype(BF)
                for a in range(8)
            ]
            out = exchange(mixed)
            for g in range(8):
                m_own[t * 8 + g] = out[g]

    def send_halo(i, j):
        @pl.when(has_next)
        def _():
            x_copy(i).start()

        @pl.when(has_prev)
        def _():
            m_copy(j).start()

    def wait_halo(i, j):
        @pl.when(has_prev)
        def _():
            x_copy(i).wait_recv()

        @pl.when(has_next)
        def _():
            m_copy(j).wait_recv()

    def to_peer(src, dst, kind, peer):
        return pltpu.make_async_remote_copy(
            src_ref=src,
            dst_ref=dst,
            send_sem=peer_sem.at[kind],
            recv_sem=peer_sem.at[kind + 4],
            device_id={"zero": peer},
            device_id_type=MESH,
        )

    def all_shares():
        ref = shares.at[pl.ds(1, ZERO - 1)]
        return to_peer(ref, ref, 2, ahead(1))

    row = pl.ds(0, 1)

    def all_rows():
        ref = squares.at[pl.ds(1, ZERO - 1), row]
        return to_peer(ref, ref, 3, ahead(1))

    arrange(0, CHUNKS - 1)
    pl.semaphore_wait(barrier, ZERO - 1 + len(mates))
    send_halo(0, CHUNKS - 1)

    def to_sibling():
        return to_peer(filt, sibling, 0, me + 1 - 2 * core)

    def to_chip(d):
        return to_peer(taps.at[chip], taps.at[chip], 1, lax.rem(me + 2 * d, ZERO))

    def all_chips():
        ref = taps.at[pl.ds(1, ZERO // 2 - 1)]
        return to_peer(ref, ref, 1, ahead(2))

    for i, hbm in enumerate((filt_hbm, one_hbm, two_hbm)):
        load_small(hbm, i).wait()
    to_sibling().start()

    @pl.loop(1, HALF)
    def _(i):
        arrange(i, CHUNKS - 1 - i)
        send_halo(i, CHUNKS - 1 - i)

    to_sibling().wait_recv()
    own_taps, other_taps = filt[...], sibling[...]
    first_core = core == 0
    taps[chip] = jnp.concatenate(
        [
            jnp.where(first_core, own_taps, other_taps),
            jnp.where(first_core, other_taps, own_taps),
        ],
        axis=0,
    ).astype(BF)

    @pl.loop(1, ZERO // 2)
    def _(d):
        to_chip(d).start()

    @pl.loop(HALF, EARLY)
    def _(i):
        arrange(i, CHUNKS - 1 - i)
        send_halo(i, CHUNKS - 1 - i)

    @pl.loop(EARLY, CHUNKS)
    def _(i):
        arrange(i, CHUNKS - 1 - i)

    def x_windows(n):
        return windows(x_prev[n], x_own[n])

    def m_windows(n):
        return windows(m_own[n], m_next[n])

    def lag_tile(t, wins_of, own, forward):
        sums = []
        for g in range(0, 8, 2):
            n = t * 8 + g
            lags = pair_lags([own[n], own[n + 1]], [wins_of(n), wins_of(n + 1)])
            sums += [diagonal(v, forward) for v in lags]
        grads[t] = jnp.sum(jnp.stack(sums), axis=1)

    def send_share(t):
        @pl.when(t != me)
        def _():
            d = lax.rem(t - me + ZERO, ZERO)
            to_peer(grads.at[t], shares.at[d], 2, t).start()

    @pl.loop(0, HALF)
    def _(i):
        j = CHUNKS - 1 - i
        wait_halo(i, j)

        for u in range(TILES):
            lag_tile(i * TILES + u, x_windows, m_own, True)
            lag_tile(j * TILES + u, m_windows, x_own, False)

        for u in range(TILES):
            send_share(i * TILES + u)
            send_share(j * TILES + u)

    @pl.loop(EARLY, CHUNKS)
    def _(i):
        send_halo(i, CHUNKS - 1 - i)

    all_chips().wait_recv()

    def conv_tile(t, rows, wins_of, taps_of):
        conv = []
        for g in range(0, 8, 2):
            n = t * 8 + g
            conv += pair_convolved(
                [taps_of(rows[g + e : g + e + 1]) for e in range(2)], [wins_of(n), wins_of(n + 1)]
            )
        return exchange(conv)

    def store(vmem, hbm, sem, i):
        return pltpu.make_async_copy(vmem.at[:, wide(i)], hbm.at[0, :, wide(i)], sem.at[i])

    def convolve(i):
        j = CHUNKS - 1 - i
        x_taps, m_taps = taps[i].astype(F32), taps[j].astype(F32)
        for u in range(TILES):
            t = i * TILES + u
            out = conv_tile(t, x_taps[8 * u : 8 * u + 8], x_windows, forward_taps)
            for a in range(8):
                at = (slice(16 * a, 16 * a + 16), tile_of(t))
                qg[at] = (ct_in[at].astype(F32) * out[a].astype(F32)).astype(BF)
            t = j * TILES + u
            out = conv_tile(t, m_taps[8 * u : 8 * u + 8], m_windows, backward_taps)
            for a in range(8):
                ig[16 * a : 16 * a + 16, tile_of(t)] = out[a]
        store(qg, qg_hbm, qg_st, i).start()
        store(ig, ig_hbm, ig_st, j).start()

    def convolve_late(i):
        wait_halo(i, CHUNKS - 1 - i)
        convolve(i)

    @pl.loop(0, RS_BESIDE)
    def _(i):
        convolve(i)

    count = jnp.full((8, 128), step_ref[0], jnp.int32).astype(F32) + 1.0
    rate = LEARN_RATE / (1.0 - jnp.exp(count * math.log(BETA_ONE)))
    spread = 1.0 / (1.0 - jnp.exp(count * math.log(BETA_TWO)))
    all_shares().wait_recv()
    shares[0] = grads[me]
    grad = jnp.sum(shares[...], axis=0)
    squares[0] = jnp.broadcast_to(jnp.sum(grad * grad, axis=0, keepdims=True), (8, 128))

    @pl.loop(1, ZERO)
    def _(d):
        to_peer(squares.at[0, row], squares.at[d, row], 3, ahead(d)).start()

    @pl.loop(RS_BESIDE, HALF)
    def _(i):
        convolve(i)

    @pl.loop(HALF, NORM_BESIDE)
    def _(i):
        convolve_late(i)

    all_rows().wait_recv()
    total = jnp.sum(squares[:, 0, :], axis=(0, 1), keepdims=True)
    norm = jnp.sqrt(jnp.broadcast_to(total, (8, 128)))
    clipped = grad * jnp.minimum(1.0, CLIP_NORM / (norm + 1e-06))
    moment_one = BETA_ONE * one[...] + (1.0 - BETA_ONE) * clipped
    moment_two = BETA_TWO * two[...] + (1.0 - BETA_TWO) * clipped * clipped
    stepped[...] = filt[...] - rate * moment_one / (jnp.sqrt(moment_two * spread) + ADAM_EPS)

    def to_mate(b):
        return pltpu.make_async_remote_copy(
            src_ref=stepped,
            dst_ref=partners.at[b],
            send_sem=p_snd.at[b],
            recv_sem=p_rcv.at[b],
            device_id={"rep": mates[b]},
            device_id_type=MESH,
        )

    for b in range(3):
        to_mate(b).start()

    @pl.loop(NORM_BESIDE, CHUNKS)
    def _(i):
        convolve_late(i)

    for b in range(3):
        to_mate(b).wait_recv()
    bit = lax.rem(jnp.full((8, 128), step_ref[0], jnp.int32), 3)
    partner = jnp.where(bit == 0, partners[0], jnp.where(bit == 1, partners[1], partners[2]))
    renewed[...] = 0.5 * (stepped[...] + partner)
    result = pltpu.make_async_copy(renewed, new_hbm.at[0], small_sem.at[3])
    result.start()

    for b in range(3):
        to_mate(b).wait_send()
    to_sibling().wait_send()
    all_chips().wait_send()
    all_shares().wait_send()
    all_rows().wait_send()

    @pl.loop(0, CHUNKS)
    def _(i):
        store(qg, qg_hbm, qg_st, i).wait()
        store(ig, ig_hbm, ig_st, i).wait()

        @pl.when(has_next)
        def _():
            x_copy(i).wait_send()

        @pl.when(has_prev)
        def _():
            m_copy(i).wait_send()

    result.wait()


def on_device(gated_input, query_gate, cotangent, filters, first_moment, second_moment, step_index):
    anywhere = pl.BlockSpec(memory_space=pl.ANY)
    dma = pltpu.SemaphoreType.DMA
    _, rows, channels = gated_input.shape
    groups = channels // 16
    natural = pltpu.VMEM((rows, channels), BF)
    grouped = pltpu.VMEM((groups, 16, 128), BF)
    shards = pltpu.VMEM((ZERO, 8, 128), F32)
    return pl.pallas_call(
        kernel,
        name="hyena_step",
        out_shape=[
            jax.ShapeDtypeStruct(gated_input.shape, BF),
            jax.ShapeDtypeStruct(gated_input.shape, BF),
            jax.ShapeDtypeStruct(filters.shape, F32),
        ],
        in_specs=[anywhere] * 6 + [pl.BlockSpec(memory_space=pltpu.SMEM)],
        out_specs=[anywhere] * 3,
        scratch_shapes=[natural] * 3
        + [grouped] * 4
        + [natural] * 2
        + [pltpu.VMEM((ZERO // 2, 16, 128), BF)]
        + [shards] * 3
        + [pltpu.VMEM((6, 8, 128), F32), pltpu.VMEM((3, 8, 128), F32)]
        + [dma((CHUNKS,))] * 9
        + [dma((4,)), dma((3,)), dma((3,)), dma((8,))],
        compiler_params=pltpu.CompilerParams(
            collective_id=0, has_side_effects=True, vmem_limit_bytes=62 << 20
        ),
        cost_estimate=pl.CostEstimate(flops=4 << 30, bytes_accessed=8 << 20, transcendentals=0),
    )(gated_input, query_gate, cotangent, filters, first_moment, second_moment, step_index)


def solution(mesh):
    split = P("rep", "zero", None)
    return jax.shard_map(
        on_device,
        mesh=mesh,
        in_specs=(split,) * 6 + (P(),),
        out_specs=(split,) * 3,
        check_vma=False,
    )
```

time: 54.6 us -> 41.2 us (0.75)
  Pallas kernels: 44.7 us -> 35.8 us
  local copies, waits for them, and re-layouts: 8.26 us -> 3.95 us
    pallas_call x1, Pallas kernels: 44.7 us -> 35.8 us  [on_device(): pl.pallas_call(kernel, name='hyena_step', out_shape=[jax.ShapeDtypeStruct...]
    unnamed x15 -> x7, local copies, waits for them, and re-layouts: 8.26 us -> 3.95 us
where the time goes in v2:
time: 41.2 us; the launch traced here: 41.1 us
  Pallas kernels  35.8 us (87%)
  local copies, waits for them, and re-layouts  3.95 us (10%)
  between operations  1.3 us (3%)
    pallas_call x1, Pallas kernels, on_device(): pl.pallas_call(kernel, name='hyena_step', out_shape=[jax.ShapeDtypeStruct...  35.8 us
    unnamed x7, local copies, waits for them, and re-layouts  3.95 us

profile of v2, /device:TPU:1, one launch (start us, length us, event | category | flops | bytes accessed | tf_op | source)
XLA Modules:
  0.0 41.1 jit_solution(6098739949636846824)
XLA Ops:
  1.3 35.8 %hyena_step.1 = (bf16[1,128,4096]{2,1,0:T(8,128)(2,1)}, bf16[1,128,4096]{2,1,0:T(8,128)(2,1)}, f32[1,8,128]{2,1,0:T(8,128)}) custom-call(bf16[1,128,4096]{2,1,0:T(8,128)(2,1)} %x_hbm.1, bf16[1,128,4096]{2,1,0:T(8,128)(2,1)} %gate_hbm.1, bf16[1,128,4096]{2,1,0:T(8,128)(2,1)} %ct_hbm.1, f32[1,8,128]{2,1,0:T(8,128)} %filt_hbm.1, f32[1,8,128]{2,1,0:T(8,128)} %one_hbm.1, ...), custom_call_target="tpu_custom_call" | custom-call | flops 4294967296 | bytes 8388608 | tf_op jit(solution)/shard_map/hyena_step/pallas_call | solution.py:489
  37.1 0.0 copy-start
  37.1 2.4 %copy.14 = bf16[1,128,4096]{2,1,0:T(8,128)(2,1)} copy(bf16[1,128,4096]{2,1,0:T(8,128)(2,1)} %get-tuple-element.6) | data formatting | bytes 2097152
  39.5 0.0 copy-done
  39.5 0.0 copy-start.1
  39.5 1.0 %copy.15 = bf16[1,128,4096]{2,1,0:T(8,128)(2,1)} copy(bf16[1,128,4096]{2,1,0:T(8,128)(2,1)S(1)} %copy-done) | data formatting | bytes 2097152
  40.5 0.0 copy-done.1
  40.5 0.6 %copy.16 = f32[1,8,128]{2,1,0:T(8,128)} copy(f32[1,8,128]{2,1,0:T(8,128)S(1)} %copy-done.1) | data formatting | bytes 8192
Async XLA Ops:
  37.1 2.4 %copy-start = (bf16[1,128,4096]{2,1,0:T(8,128)(2,1)S(1)}, bf16[1,128,4096]{2,1,0:T(8,128)(2,1)}, u32[]{:S(2)}) copy-start(bf16[1,128,4096]{2,1,0:T(8,128)(2,1)} %get-tuple-element.7) | copy-start | bytes 3145732
  39.5 1.0 %copy-start.1 = (f32[1,8,128]{2,1,0:T(8,128)S(1)}, f32[1,8,128]{2,1,0:T(8,128)}, u32[]{:S(2)}) copy-start(f32[1,8,128]{2,1,0:T(8,128)} %get-tuple-element.8) | copy-start | bytes 12292

commit v3 on v2

--- a/solution.py
+++ b/solution.py
@@ -23,9 +23,7 @@
 HALF = CHUNKS // 2
 WIDE = TILES * 128
 GROUPS = TILES * 8
-EARLY = 8
-RS_BESIDE = 5
-NORM_BESIDE = 11
+RS_BESIDE = 4
 
 
 def lane_ids():
@@ -108,11 +106,9 @@
     x_hbm,
     gate_hbm,
     ct_hbm,
-    filt_hbm,
-    one_hbm,
-    two_hbm,
+    small_hbm,
     step_ref,
-    qg_hbm,
+    conv_hbm,
     ig_hbm,
     new_hbm,
     x_in,
@@ -122,14 +118,16 @@
     m_own,
     x_prev,
     m_next,
-    qg,
+    conv,
     ig,
     taps,
     grads,
     shares,
-    squares,
+    near,
+    far,
     small,
-    partners,
+    mate_small,
+    mate_grad,
     x_ld,
     gate_ld,
     ct_ld,
@@ -137,11 +135,12 @@
     x_rcv,
     m_snd,
     m_rcv,
-    qg_st,
+    conv_st,
     ig_st,
     small_sem,
     p_snd,
     p_rcv,
+    far_sem,
     peer_sem,
 ):
     me = lax.axis_index("zero")
@@ -153,12 +152,40 @@
         rep + 2 - 4 * lax.rem(lax.div(rep, 2), 2),
         lax.rem(rep + 4, 8),
     ]
-    filt, one, two, stepped, sibling, renewed = (small.at[i] for i in range(6))
+    filt, one, two, own_grad, sibling, renewed = (small.at[i] for i in range(6))
+    block, place = lax.div(me, 8), lax.rem(me, 8)
     core = lax.rem(me, 2)
     chip = lax.div(me, 2)
 
     def ahead(d):
         return lax.rem(me + d, ZERO)
+
+    last = CHUNKS - 1
+    rest = (CHUNKS - 1) * WIDE
+
+    def load(hbm, vmem, sem, which, at, size):
+        cols = pl.ds(at, size)
+        return pltpu.make_async_copy(hbm.at[0, :, cols], vmem.at[:, cols], sem.at[which])
+
+    def load_first():
+        return [
+            load(x_hbm, x_in, x_ld, 0, 0, WIDE),
+            load(ct_hbm, ct_in, ct_ld, 0, rest, WIDE),
+            load(gate_hbm, gate_in, gate_ld, 0, rest, WIDE),
+        ]
+
+    def load_rest():
+        return [
+            load(x_hbm, x_in, x_ld, 1, WIDE, rest),
+            load(ct_hbm, ct_in, ct_ld, 1, 0, rest),
+            load(gate_hbm, gate_in, gate_ld, 1, 0, rest),
+        ]
+
+    def load_small():
+        return [pltpu.make_async_copy(small_hbm, small.at[pl.ds(0, 3)], small_sem.at[0])]
+
+    for copy in load_first() + load_rest() + load_small():
+        copy.start()
 
     barrier = pltpu.get_barrier_semaphore()
 
@@ -167,25 +194,9 @@
         pl.semaphore_signal(barrier, 1, device_id={"zero": ahead(d)}, device_id_type=MESH)
 
     for mate in mates:
-        pl.semaphore_signal(barrier, 1, device_id={"rep": mate}, device_id_type=MESH)
-
-    def wide(i):
-        return pl.ds(pl.multiple_of(i * WIDE, WIDE), WIDE)
-
-    def load(hbm, vmem, sem, i):
-        return pltpu.make_async_copy(hbm.at[0, :, wide(i)], vmem.at[:, wide(i)], sem.at[i])
-
-    def load_small(hbm, i):
-        return pltpu.make_async_copy(hbm.at[0], small.at[i], small_sem.at[i])
-
-    for i, hbm in enumerate((filt_hbm, one_hbm, two_hbm)):
-        load_small(hbm, i).start()
-
-    @pl.loop(0, CHUNKS)
-    def _(i):
-        load(x_hbm, x_in, x_ld, i).start()
-        load(ct_hbm, ct_in, ct_ld, CHUNKS - 1 - i).start()
-        load(gate_hbm, gate_in, gate_ld, CHUNKS - 1 - i).start()
+        for d in range(4):
+            other = {"rep": mate, "zero": lax.rem(me + 8 * d, ZERO)}
+            pl.semaphore_signal(barrier, 1, device_id=other, device_id_type=MESH)
 
     @pl.when(me == 0)
     def _():
@@ -222,9 +233,6 @@
         return pl.ds(pl.multiple_of(t * 128, 128), 128)
 
     def arrange(i, j):
-        load(x_hbm, x_in, x_ld, i).wait()
-        load(ct_hbm, ct_in, ct_ld, j).wait()
-        load(gate_hbm, gate_in, gate_ld, j).wait()
         for u in range(TILES):
             t = i * TILES + u
             out = exchange([x_in[16 * a : 16 * a + 16, tile_of(t)] for a in range(8)])
@@ -276,13 +284,51 @@
 
     row = pl.ds(0, 1)
 
-    def all_rows():
-        ref = squares.at[pl.ds(1, ZERO - 1), row]
+    def to_near(d):
+        return to_peer(near.at[0, row], near.at[d, row], 3, block * 8 + lax.rem(place + d, 8))
+
+    def all_near():
+        ref = near.at[pl.ds(1, 7), row]
         return to_peer(ref, ref, 3, ahead(1))
 
-    arrange(0, CHUNKS - 1)
-    pl.semaphore_wait(barrier, ZERO - 1 + len(mates))
-    send_halo(0, CHUNKS - 1)
+    def to_far(slot, src, dst):
+        other = {"zero": lax.rem(me + 8 * (slot % 4), ZERO)}
+        if slot >= 4:
+            other["rep"] = mates[slot // 4 - 1]
+        return pltpu.make_async_remote_copy(
+            src_ref=src,
+            dst_ref=dst,
+            send_sem=far_sem.at[0],
+            recv_sem=far_sem.at[1],
+            device_id=other,
+            device_id_type=MESH,
+        )
+
+    def all_far():
+        ref = far.at[pl.ds(1, 15), row]
+        return to_far(1, ref, ref)
+
+    def to_mate(b, src, dst, kind):
+        return pltpu.make_async_remote_copy(
+            src_ref=src,
+            dst_ref=dst,
+            send_sem=p_snd.at[3 * kind + b],
+            recv_sem=p_rcv.at[3 * kind + b],
+            device_id={"rep": mates[b]},
+            device_id_type=MESH,
+        )
+
+    def params_to_mate(b):
+        return to_mate(b, small.at[pl.ds(0, 3)], mate_small.at[b], 0)
+
+    def grad_to_mate(b):
+        return to_mate(b, own_grad, mate_grad.at[b], 1)
+
+    for copy in load_first():
+        copy.wait()
+    arrange(0, last)
+    pl.semaphore_wait(barrier, ZERO - 1 + 4 * len(mates))
+    send_halo(0, last)
 
     def to_sibling():
         return to_peer(filt, sibling, 0, me + 1 - 2 * core)
@@ -294,8 +340,8 @@
         ref = taps.at[pl.ds(1, ZERO // 2 - 1)]
         return to_peer(ref, ref, 1, ahead(2))
 
-    for i, hbm in enumerate((filt_hbm, one_hbm, two_hbm)):
-        load_small(hbm, i).wait()
+    for copy in load_rest() + load_small():
+        copy.wait()
     to_sibling().start()
 
     @pl.loop(1, HALF)
@@ -318,12 +364,10 @@
     def _(d):
         to_chip(d).start()
 
-    @pl.loop(HALF, EARLY)
-    def _(i):
-        arrange(i, CHUNKS - 1 - i)
-        send_halo(i, CHUNKS - 1 - i)
-
-    @pl.loop(EARLY, CHUNKS)
+    for b in range(3):
+        params_to_mate(b).start()
+
+    @pl.loop(HALF, CHUNKS)
     def _(i):
         arrange(i, CHUNKS - 1 - i)
 
@@ -360,23 +404,31 @@
             send_share(i * TILES + u)
             send_share(j * TILES + u)
 
-    @pl.loop(EARLY, CHUNKS)
-    def _(i):
-        send_halo(i, CHUNKS - 1 - i)
-
     all_chips().wait_recv()
 
     def conv_tile(t, rows, wins_of, taps_of):
-        conv = []
+        done = []
         for g in range(0, 8, 2):
             n = t * 8 + g
-            conv += pair_convolved(
+            done += pair_convolved(
                 [taps_of(rows[g + e : g + e + 1]) for e in range(2)], [wins_of(n), wins_of(n + 1)]
             )
-        return exchange(conv)
-
-    def store(vmem, hbm, sem, i):
-        return pltpu.make_async_copy(vmem.at[:, wide(i)], hbm.at[0, :, wide(i)], sem.at[i])
+        return exchange(done)
+
+    cuts = (0, RS_BESIDE, HALF, CHUNKS - 2, CHUNKS)
+
+    def stores(part):
+        low, high = cuts[part] * WIDE, cuts[part + 1] * WIDE
+        x_cols = pl.ds(low, high - low)
+        m_cols = pl.ds(CHUNKS * WIDE - high, high - low)
+        return [
+            pltpu.make_async_copy(conv.at[:, x_cols], conv_hbm.at[0, :, x_cols], conv_st.at[part]),
+            pltpu.make_async_copy(ig.at[:, m_cols], ig_hbm.at[0, :, m_cols], ig_st.at[part]),
+        ]
+
+    def store(part):
+        for copy in stores(part):
+            copy.start()
 
     def convolve(i):
         j = CHUNKS - 1 - i
@@ -386,13 +438,11 @@
             out = conv_tile(t, x_taps[8 * u : 8 * u + 8], x_windows, forward_taps)
             for a in range(8):
                 at = (slice(16 * a, 16 * a + 16), tile_of(t))
-                qg[at] = (ct_in[at].astype(F32) * out[a].astype(F32)).astype(BF)
+                conv[at] = out[a]
             t = j * TILES + u
             out = conv_tile(t, m_taps[8 * u : 8 * u + 8], m_windows, backward_taps)
             for a in range(8):
                 ig[16 * a : 16 * a + 16, tile_of(t)] = out[a]
-        store(qg, qg_hbm, qg_st, i).start()
-        store(ig, ig_hbm, ig_st, j).start()
 
     def convolve_late(i):
         wait_halo(i, CHUNKS - 1 - i)
@@ -400,73 +450,53 @@
 
     @pl.loop(0, RS_BESIDE)
     def _(i):
+        send_halo(HALF + i, last - HALF - i)
         convolve(i)
 
+    store(0)
     count = jnp.full((8, 128), step_ref[0], jnp.int32).astype(F32) + 1.0
     rate = LEARN_RATE / (1.0 - jnp.exp(count * math.log(BETA_ONE)))
     spread = 1.0 / (1.0 - jnp.exp(count * math.log(BETA_TWO)))
     all_shares().wait_recv()
     shares[0] = grads[me]
     grad = jnp.sum(shares[...], axis=0)
-    squares[0] = jnp.broadcast_to(jnp.sum(grad * grad, axis=0, keepdims=True), (8, 128))
-
-    @pl.loop(1, ZERO)
-    def _(d):
-        to_peer(squares.at[0, row], squares.at[d, row], 3, ahead(d)).start()
+    own_grad[...] = grad
+    near[0] = jnp.broadcast_to(jnp.sum(grad * grad, axis=0, keepdims=True), (8, 128))
+    for d in range(1, 8):
+        to_near(d).start()
+    for b in range(3):
+        grad_to_mate(b).start()
 
     @pl.loop(RS_BESIDE, HALF)
     def _(i):
+        send_halo(HALF + i, last - HALF - i)
         convolve(i)
 
-    @pl.loop(HALF, NORM_BESIDE)
+    all_near().wait_recv()
+    near_sum = jnp.sum(near[:, 0, :], axis=0, keepdims=True)
+    far[0] = jnp.broadcast_to(near_sum, (8, 128))
+    for slot in range(1, 16):
+        to_far(slot, far.at[0, row], far.at[slot, row]).start()
+    store(1)
+
+    @pl.loop(HALF, CHUNKS - 2)
     def _(i):
         convolve_late(i)
 
-    all_rows().wait_recv()
-    total = jnp.sum(squares[:, 0, :], axis=(0, 1), keepdims=True)
-    norm = jnp.sqrt(jnp.broadcast_to(total, (8, 128)))
-    clipped = grad * jnp.minimum(1.0, CLIP_NORM / (norm + 1e-06))
-    moment_one = BETA_ONE * one[...] + (1.0 - BETA_ONE) * clipped
-    moment_two = BETA_TWO * two[...] + (1.0 - BETA_TWO) * clipped * clipped
-    stepped[...] = filt[...] - rate * moment_one / (jnp.sqrt(moment_two * spread) + ADAM_EPS)
-
-    def to_mate(b):
-        return pltpu.make_async_remote_copy(
-            src_ref=stepped,
-            dst_ref=partners.at[b],
-            send_sem=p_snd.at[b],
-            recv_sem=p_rcv.at[b],
-            device_id={"rep": mates[b]},
-            device_id_type=MESH,
-        )
-
-    for b in range(3):
-        to_mate(b).start()
-
-    @pl.loop(NORM_BESIDE, CHUNKS)
+    store(2)
+
+    @pl.loop(CHUNKS - 2, CHUNKS)
     def _(i):
         convolve_late(i)
 
-    for b in range(3):
-        to_mate(b).wait_recv()
-    bit = lax.rem(jnp.full((8, 128), step_ref[0], jnp.int32), 3)
-    partner = jnp.where(bit == 0, partners[0], jnp.where(bit == 1, partners[1], partners[2]))
-    renewed[...] = 0.5 * (stepped[...] + partner)
-    result = pltpu.make_async_copy(renewed, new_hbm.at[0], small_sem.at[3])
-    result.start()
-
-    for b in range(3):
-        to_mate(b).wait_send()
+    store(3)
     to_sibling().wait_send()
     all_chips().wait_send()
     all_shares().wait_send()
-    all_rows().wait_send()
+    all_near().wait_send()
 
     @pl.loop(0, CHUNKS)
     def _(i):
-        store(qg, qg_hbm, qg_st, i).wait()
-        store(ig, ig_hbm, ig_st, i).wait()
-
         @pl.when(has_next)
         def _():
             x_copy(i).wait_send()
@@ -475,6 +505,43 @@
         def _():
             m_copy(i).wait_send()
 
+    for b in range(3):
+        params_to_mate(b).wait()
+        grad_to_mate(b).wait()
+    bit = lax.rem(jnp.full((8, 128), step_ref[0], jnp.int32), 3)
+
+    def picked(of):
+        return jnp.where(bit == 0, of(0), jnp.where(bit == 1, of(1), of(2)))
+
+    mate_values = [picked(lambda b: mate_small[b, i]) for i in range(3)]
+    mate_values.append(picked(lambda b: mate_grad[b]))
+
+    def stepped(values, squares):
+        weights, first, second, gradient = values
+        total = jnp.sum(squares, axis=(0, 1), keepdims=True)
+        norm = jnp.sqrt(jnp.broadcast_to(total, (8, 128)))
+        clipped = gradient * jnp.minimum(1.0, CLIP_NORM / (norm + 1e-06))
+        moment_one = BETA_ONE * first + (1.0 - BETA_ONE) * clipped
+        moment_two = BETA_TWO * second + (1.0 - BETA_TWO) * clipped * clipped
+        return weights - rate * moment_one / (jnp.sqrt(moment_two * spread) + ADAM_EPS)
+
+    all_far().wait()
+    low, high = far[0:8, 0, :], far[8:16, 0, :]
+    four = lax.broadcasted_iota(jnp.int32, (8, 128), 0) < 4
+    none = jnp.zeros((8, 128), F32)
+    own_squares = jnp.where(four, low, none)
+    mate_squares = jnp.where(
+        bit == 0,
+        jnp.where(four, none, low),
+        jnp.where((bit == 1) == four, high, none),
+    )
+    own = stepped([filt[...], one[...], two[...], grad], own_squares)
+    renewed[...] = 0.5 * (own + stepped(mate_values, mate_squares))
+    result = pltpu.make_async_copy(renewed, new_hbm.at[0], small_sem.at[1])
+    result.start()
+    for part in range(4):
+        for copy in stores(part):
+            copy.wait()
     result.wait()
 
 
@@ -486,7 +553,8 @@
     natural = pltpu.VMEM((rows, channels), BF)
     grouped = pltpu.VMEM((groups, 16, 128), BF)
     shards = pltpu.VMEM((ZERO, 8, 128), F32)
-    return pl.pallas_call(
+    shard = jnp.concatenate([filters, first_moment, second_moment], axis=0)
+    conv, input_grad, new_filters = pl.pallas_call(
         kernel,
         name="hyena_step",
         out_shape=[
@@ -494,21 +562,27 @@
             jax.ShapeDtypeStruct(gated_input.shape, BF),
             jax.ShapeDtypeStruct(filters.shape, F32),
         ],
-        in_specs=[anywhere] * 6 + [pl.BlockSpec(memory_space=pltpu.SMEM)],
+        in_specs=[anywhere] * 4 + [pl.BlockSpec(memory_space=pltpu.SMEM)],
         out_specs=[anywhere] * 3,
         scratch_shapes=[natural] * 3
         + [grouped] * 4
         + [natural] * 2
         + [pltpu.VMEM((ZERO // 2, 16, 128), BF)]
-        + [shards] * 3
-        + [pltpu.VMEM((6, 8, 128), F32), pltpu.VMEM((3, 8, 128), F32)]
-        + [dma((CHUNKS,))] * 9
-        + [dma((4,)), dma((3,)), dma((3,)), dma((8,))],
+        + [shards] * 2
+        + [pltpu.VMEM((8, 8, 128), F32), pltpu.VMEM((16, 8, 128), F32)]
+        + [pltpu.VMEM((6, 8, 128), F32), pltpu.VMEM((3, 3, 8, 128), F32)]
+        + [pltpu.VMEM((3, 8, 128), F32)]
+        + [dma((2,))] * 3
+        + [dma((CHUNKS,))] * 4
+        + [dma((4,))] * 2
+        + [dma((2,)), dma((6,)), dma((6,)), dma((2,)), dma((8,))],
         compiler_params=pltpu.CompilerParams(
-            collective_id=0, has_side_effects=True, vmem_limit_bytes=62 << 20
+            collective_id=0, has_side_effects=True, vmem_limit_bytes=51 << 20
         ),
         cost_estimate=pl.CostEstimate(flops=4 << 30, bytes_accessed=8 << 20, transcendentals=0),
-    )(gated_input, query_gate, cotangent, filters, first_moment, second_moment, step_index)
+    )(gated_input, query_gate, cotangent, shard, step_index)
+    query_grad = (cotangent.astype(F32) * conv.astype(F32)).astype(BF)
+    return query_grad, input_grad, new_filters
 
 
 def solution(mesh):

time: 41.2 us -> 39.4 us (0.956)
  local copies, waits for them, and re-layouts: 3.95 us -> 1.57 us
  other arithmetic: 0 us -> 1.95 us
  Pallas kernels: 35.8 us -> 34.4 us
    unnamed x7 -> x4, local copies, waits for them, and re-layouts: 3.95 us -> 1.57 us
    pallas_call x1, Pallas kernels: 35.8 us -> 34.4 us  [on_device(): pl.pallas_call(kernel, name='hyena_step', out_shape=[jax.ShapeDtypeStruct...]
    convert_element_type x0 -> x1, other arithmetic: none -> 1.22 us  [on_device(): query_grad = (cotangent.astype(F32) * conv.astype(F32)).astype(BF)]
    concatenate x0 -> x1, other arithmetic: none -> 0.72 us  [on_device(): shard = jnp.concatenate([filters, first_moment, second_moment], axis=0)]
where the time goes in v3:
time: 39.4 us; the launch traced here: 39.3 us
  Pallas kernels  34.4 us (87%)
  other arithmetic  1.95 us (5%)
  local copies, waits for them, and re-layouts  1.57 us (4%)
  between operations  1.3 us (3%)
    pallas_call x1, Pallas kernels, on_device(): pl.pallas_call(kernel, name='hyena_step', out_shape=[jax.ShapeDtypeStruct...  34.4 us
    unnamed x4, local copies, waits for them, and re-layouts  1.57 us
    convert_element_type x1, other arithmetic, on_device(): query_grad = (cotangent.astype(F32) * conv.astype(F32)).astype(BF)  1.22 us

profile of v3, /device:TPU:1, one launch (start us, length us, event | category | flops | bytes accessed | tf_op | source)
XLA Modules:
  0.0 39.3 jit_solution(12502213244670439494)
XLA Ops:
  1.3 0.7 %pad_maximum_fusion.small_hbm = f32[3,8,128]{2,1,0:T(8,128)S(1)} fusion(f32[1,8,128]{2,1,0:T(8,128)} %param.12, f32[1,8,128]{2,1,0:T(8,128)} %param.11, f32[1,8,128]{2,1,0:T(8,128)} %param.10), kind=kLoop, calls=%fused_computation.1 | loop fusion | flops 6144 | bytes 24576 | tf_op jit(solution)/shard_map/concatenate | solution.py:556
  2.0 0.0 copy-start
  2.0 34.4 %hyena_step.1 = (bf16[1,128,4096]{2,1,0:T(8,128)(2,1)S(1)}, bf16[1,128,4096]{2,1,0:T(8,128)(2,1)S(1)}, f32[1,8,128]{2,1,0:T(8,128)S(1)}) custom-call(bf16[1,128,4096]{2,1,0:T(8,128)(2,1)} %x_hbm.1, bf16[1,128,4096]{2,1,0:T(8,128)(2,1)} %gate_hbm.1, bf16[1,128,4096]{2,1,0:T(8,128)(2,1)} %ct_hbm.1, f32[3,8,128]{2,1,0:T(8,128)S(1)} %pad_maximum_fusion.small_hbm, ...), custom_call_target="tpu_custom_call" | custom-call | flops 4294967296 | bytes 8388608 | tf_op jit(solution)/shard_map/hyena_step/pallas_call | solution.py:557
  36.5 0.0 copy-done
  36.5 1.2 %multiply_convert_fusion = bf16[1,128,4096]{2,1,0:T(8,128)(2,1)} fusion(bf16[1,128,4096]{2,1,0:T(8,128)(2,1)S(1)} %get-tuple-element.6, bf16[1,128,4096]{2,1,0:T(8,128)(2,1)S(1)} %copy-done), kind=kLoop, calls=%fused_computation | loop fusion | flops 2097152 | bytes 3145728 | tf_op jit(solution)/shard_map/convert_element_type | solution.py:584
  37.7 1.0 %copy.13 = bf16[1,128,4096]{2,1,0:T(8,128)(2,1)} copy(bf16[1,128,4096]{2,1,0:T(8,128)(2,1)S(1)} %get-tuple-element.13) | data formatting | bytes 2097152
  38.7 0.6 %copy.14 = f32[1,8,128]{2,1,0:T(8,128)} copy(f32[1,8,128]{2,1,0:T(8,128)S(1)} %get-tuple-element.14) | data formatting | bytes 8192
Async XLA Ops:
  2.0 34.5 %copy-start = (bf16[1,128,4096]{2,1,0:T(8,128)(2,1)S(1)}, bf16[1,128,4096]{2,1,0:T(8,128)(2,1)}, u32[]{:S(2)}) copy-start(bf16[1,128,4096]{2,1,0:T(8,128)(2,1)} %ct_hbm.1) | copy-start | bytes 3145732

commit v4 on v3

--- a/solution.py
+++ b/solution.py
@@ -108,9 +108,9 @@
     ct_hbm,
     small_hbm,
     step_ref,
-    conv_hbm,
-    ig_hbm,
-    new_hbm,
+    conv,
+    ig,
+    new_ref,
     x_in,
     gate_in,
     ct_in,
@@ -118,8 +118,6 @@
     m_own,
     x_prev,
     m_next,
-    conv,
-    ig,
     taps,
     grads,
     shares,
@@ -127,7 +125,6 @@
     far,
     small,
     mate_small,
-    mate_grad,
     x_ld,
     gate_ld,
     ct_ld,
@@ -135,8 +132,6 @@
     x_rcv,
     m_snd,
     m_rcv,
-    conv_st,
-    ig_st,
     small_sem,
     p_snd,
     p_rcv,
@@ -152,7 +147,7 @@
         rep + 2 - 4 * lax.rem(lax.div(rep, 2), 2),
         lax.rem(rep + 4, 8),
     ]
-    filt, one, two, own_grad, sibling, renewed = (small.at[i] for i in range(6))
+    filt, one, two, own_grad, sibling = (small.at[i] for i in range(5))
     block, place = lax.div(me, 8), lax.rem(me, 8)
     core = lax.rem(me, 2)
     chip = lax.div(me, 2)
@@ -308,21 +303,15 @@
         ref = far.at[pl.ds(1, 15), row]
         return to_far(1, ref, ref)
 
-    def to_mate(b, src, dst, kind):
+    def to_mate(b):
         return pltpu.make_async_remote_copy(
-            src_ref=src,
-            dst_ref=dst,
-            send_sem=p_snd.at[3 * kind + b],
-            recv_sem=p_rcv.at[3 * kind + b],
+            src_ref=small.at[pl.ds(0, 4)],
+            dst_ref=mate_small.at[b],
+            send_sem=p_snd.at[b],
+            recv_sem=p_rcv.at[b],
             device_id={"rep": mates[b]},
             device_id_type=MESH,
         )
-
-    def params_to_mate(b):
-        return to_mate(b, small.at[pl.ds(0, 3)], mate_small.at[b], 0)
-
-    def grad_to_mate(b):
-        return to_mate(b, own_grad, mate_grad.at[b], 1)
 
     for copy in load_first():
         copy.wait()
@@ -364,9 +353,6 @@
     def _(d):
         to_chip(d).start()
 
-    for b in range(3):
-        params_to_mate(b).start()
-
     @pl.loop(HALF, CHUNKS)
     def _(i):
         arrange(i, CHUNKS - 1 - i)
@@ -415,21 +401,6 @@
             )
         return exchange(done)
 
-    cuts = (0, RS_BESIDE, HALF, CHUNKS - 2, CHUNKS)
-
-    def stores(part):
-        low, high = cuts[part] * WIDE, cuts[part + 1] * WIDE
-        x_cols = pl.ds(low, high - low)
-        m_cols = pl.ds(CHUNKS * WIDE - high, high - low)
-        return [
-            pltpu.make_async_copy(conv.at[:, x_cols], conv_hbm.at[0, :, x_cols], conv_st.at[part]),
-            pltpu.make_async_copy(ig.at[:, m_cols], ig_hbm.at[0, :, m_cols], ig_st.at[part]),
-        ]
-
-    def store(part):
-        for copy in stores(part):
-            copy.start()
-
     def convolve(i):
         j = CHUNKS - 1 - i
         x_taps, m_taps = taps[i].astype(F32), taps[j].astype(F32)
@@ -438,11 +409,11 @@
             out = conv_tile(t, x_taps[8 * u : 8 * u + 8], x_windows, forward_taps)
             for a in range(8):
                 at = (slice(16 * a, 16 * a + 16), tile_of(t))
-                conv[at] = out[a]
+                conv[0, *at] = out[a]
             t = j * TILES + u
             out = conv_tile(t, m_taps[8 * u : 8 * u + 8], m_windows, backward_taps)
             for a in range(8):
-                ig[16 * a : 16 * a + 16, tile_of(t)] = out[a]
+                ig[0, 16 * a : 16 * a + 16, tile_of(t)] = out[a]
 
     def convolve_late(i):
         wait_halo(i, CHUNKS - 1 - i)
@@ -453,7 +424,6 @@
         send_halo(HALF + i, last - HALF - i)
         convolve(i)
 
-    store(0)
     count = jnp.full((8, 128), step_ref[0], jnp.int32).astype(F32) + 1.0
     rate = LEARN_RATE / (1.0 - jnp.exp(count * math.log(BETA_ONE)))
     spread = 1.0 / (1.0 - jnp.exp(count * math.log(BETA_TWO)))
@@ -465,7 +435,7 @@
     for d in range(1, 8):
         to_near(d).start()
     for b in range(3):
-        grad_to_mate(b).start()
+        to_mate(b).start()
 
     @pl.loop(RS_BESIDE, HALF)
     def _(i):
@@ -477,19 +447,14 @@
     far[0] = jnp.broadcast_to(near_sum, (8, 128))
     for slot in range(1, 16):
         to_far(slot, far.at[0, row], far.at[slot, row]).start()
-    store(1)
-
     @pl.loop(HALF, CHUNKS - 2)
     def _(i):
         convolve_late(i)
 
-    store(2)
-
     @pl.loop(CHUNKS - 2, CHUNKS)
     def _(i):
         convolve_late(i)
 
-    store(3)
     to_sibling().wait_send()
     all_chips().wait_send()
     all_shares().wait_send()
@@ -506,15 +471,13 @@
             m_copy(i).wait_send()
 
     for b in range(3):
-        params_to_mate(b).wait()
-        grad_to_mate(b).wait()
+        to_mate(b).wait()
     bit = lax.rem(jnp.full((8, 128), step_ref[0], jnp.int32), 3)
 
     def picked(of):
         return jnp.where(bit == 0, of(0), jnp.where(bit == 1, of(1), of(2)))
 
-    mate_values = [picked(lambda b: mate_small[b, i]) for i in range(3)]
-    mate_values.append(picked(lambda b: mate_grad[b]))
+    mate_values = [picked(lambda b: mate_small[b, i]) for i in range(4)]
 
     def stepped(values, squares):
         weights, first, second, gradient = values
@@ -536,13 +499,7 @@
         jnp.where((bit == 1) == four, high, none),
     )
     own = stepped([filt[...], one[...], two[...], grad], own_squares)
-    renewed[...] = 0.5 * (own + stepped(mate_values, mate_squares))
-    result = pltpu.make_async_copy(renewed, new_hbm.at[0], small_sem.at[1])
-    result.start()
-    for part in range(4):
-        for copy in stores(part):
-            copy.wait()
-    result.wait()
+    new_ref[0] = 0.5 * (own + stepped(mate_values, mate_squares))
 
 
 def on_device(gated_input, query_gate, cotangent, filters, first_moment, second_moment, step_index):
@@ -563,19 +520,16 @@
             jax.ShapeDtypeStruct(filters.shape, F32),
         ],
         in_specs=[anywhere] * 4 + [pl.BlockSpec(memory_space=pltpu.SMEM)],
-        out_specs=[anywhere] * 3,
+        out_specs=[pl.BlockSpec(memory_space=pltpu.VMEM)] * 3,
         scratch_shapes=[natural] * 3
         + [grouped] * 4
-        + [natural] * 2
         + [pltpu.VMEM((ZERO // 2, 16, 128), BF)]
         + [shards] * 2
         + [pltpu.VMEM((8, 8, 128), F32), pltpu.VMEM((16, 8, 128), F32)]
-        + [pltpu.VMEM((6, 8, 128), F32), pltpu.VMEM((3, 3, 8, 128), F32)]
-        + [pltpu.VMEM((3, 8, 128), F32)]
+        + [pltpu.VMEM((5, 8, 128), F32), pltpu.VMEM((3, 4, 8, 128), F32)]
         + [dma((2,))] * 3
         + [dma((CHUNKS,))] * 4
-        + [dma((4,))] * 2
-        + [dma((2,)), dma((6,)), dma((6,)), dma((2,)), dma((8,))],
+        + [dma((1,)), dma((3,)), dma((3,)), dma((2,)), dma((8,))],
         compiler_params=pltpu.CompilerParams(
             collective_id=0, has_side_effects=True, vmem_limit_bytes=51 << 20
         ),

time: 39.4 us -> 38.9 us (0.987)
  Pallas kernels: 34.4 us -> 34 us
    pallas_call x1, Pallas kernels: 34.4 us -> 34 us  [on_device(): pl.pallas_call(kernel, name='hyena_step', out_shape=[jax.ShapeDtypeStruct...]
where the time goes in v4:
time: 38.9 us; the launch traced here: 38.8 us
  Pallas kernels  34 us (87%)
  other arithmetic  1.95 us (5%)
  local copies, waits for them, and re-layouts  1.57 us (4%)
  between operations  1.3 us (3%)
    pallas_call x1, Pallas kernels, on_device(): pl.pallas_call(kernel, name='hyena_step', out_shape=[jax.ShapeDtypeStruct...  34 us
    unnamed x4, local copies, waits for them, and re-layouts  1.57 us
    convert_element_type x1, other arithmetic, on_device(): query_grad = (cotangent.astype(F32) * conv.astype(F32)).astype(BF)  1.22 us

profile of v4, /device:TPU:1, one launch (start us, length us, event | category | flops | bytes accessed | tf_op | source)
XLA Modules:
  0.0 38.8 jit_solution(18133813989268428339)
XLA Ops:
  1.3 0.7 %pad_maximum_fusion.small_hbm = f32[3,8,128]{2,1,0:T(8,128)S(1)} fusion(f32[1,8,128]{2,1,0:T(8,128)} %param.12, f32[1,8,128]{2,1,0:T(8,128)} %param.11, f32[1,8,128]{2,1,0:T(8,128)} %param.10), kind=kLoop, calls=%fused_computation.1 | loop fusion | flops 6144 | bytes 24576 | tf_op jit(solution)/shard_map/concatenate | solution.py:513
  2.0 0.0 copy-start
  2.0 34.0 %hyena_step.1 = (bf16[1,128,4096]{2,1,0:T(8,128)(2,1)S(1)}, bf16[1,128,4096]{2,1,0:T(8,128)(2,1)S(1)}, f32[1,8,128]{2,1,0:T(8,128)S(1)}) custom-call(bf16[1,128,4096]{2,1,0:T(8,128)(2,1)} %x_hbm.1, bf16[1,128,4096]{2,1,0:T(8,128)(2,1)} %gate_hbm.1, bf16[1,128,4096]{2,1,0:T(8,128)(2,1)} %ct_hbm.1, f32[3,8,128]{2,1,0:T(8,128)S(1)} %pad_maximum_fusion.small_hbm, ...), custom_call_target="tpu_custom_call" | custom-call | flops 4294967296 | bytes 8388608 | tf_op jit(solution)/shard_map/hyena_step/pallas_call | solution.py:514
  36.0 0.0 copy-done
  36.0 1.2 %multiply_convert_fusion = bf16[1,128,4096]{2,1,0:T(8,128)(2,1)} fusion(bf16[1,128,4096]{2,1,0:T(8,128)(2,1)S(1)} %get-tuple-element.6, bf16[1,128,4096]{2,1,0:T(8,128)(2,1)S(1)} %copy-done), kind=kLoop, calls=%fused_computation | loop fusion | flops 2097152 | bytes 3145728 | tf_op jit(solution)/shard_map/convert_element_type | solution.py:538
  37.2 1.0 %copy.13 = bf16[1,128,4096]{2,1,0:T(8,128)(2,1)} copy(bf16[1,128,4096]{2,1,0:T(8,128)(2,1)S(1)} %get-tuple-element.13) | data formatting | bytes 2097152
  38.2 0.6 %copy.14 = f32[1,8,128]{2,1,0:T(8,128)} copy(f32[1,8,128]{2,1,0:T(8,128)S(1)} %get-tuple-element.14) | data formatting | bytes 8192
Async XLA Ops:
  2.0 34.0 %copy-start = (bf16[1,128,4096]{2,1,0:T(8,128)(2,1)S(1)}, bf16[1,128,4096]{2,1,0:T(8,128)(2,1)}, u32[]{:S(2)}) copy-start(bf16[1,128,4096]{2,1,0:T(8,128)(2,1)} %ct_hbm.1) | copy-start | bytes 3145732

commit v5 on v4

--- a/solution.py
+++ b/solution.py
@@ -409,7 +409,7 @@
             out = conv_tile(t, x_taps[8 * u : 8 * u + 8], x_windows, forward_taps)
             for a in range(8):
                 at = (slice(16 * a, 16 * a + 16), tile_of(t))
-                conv[0, *at] = out[a]
+                conv[0, *at] = (ct_in[at].astype(F32) * out[a].astype(F32)).astype(BF)
             t = j * TILES + u
             out = conv_tile(t, m_taps[8 * u : 8 * u + 8], m_windows, backward_taps)
             for a in range(8):
@@ -535,8 +535,7 @@
         ),
         cost_estimate=pl.CostEstimate(flops=4 << 30, bytes_accessed=8 << 20, transcendentals=0),
     )(gated_input, query_gate, cotangent, shard, step_index)
-    query_grad = (cotangent.astype(F32) * conv.astype(F32)).astype(BF)
-    return query_grad, input_grad, new_filters
+    return conv, input_grad, new_filters
 
 
 def solution(mesh):

time: 38.9 us -> 38.6 us (level)
  other arithmetic: 1.95 us -> 0.72 us
  local copies, waits for them, and re-layouts: 1.57 us -> 2.53 us
    convert_element_type x1 -> x0, other arithmetic: 1.22 us -> none  [on_device(): query_grad = (cotangent.astype(F32) * conv.astype(F32)).astype(BF)]
    unnamed x4 -> x3, local copies, waits for them, and re-layouts: 1.57 us -> 2.53 us
where the time goes in v5:
time: 38.6 us; the launch traced here: 38.5 us
  Pallas kernels  34 us (88%)
  local copies, waits for them, and re-layouts  2.53 us (7%)
  between operations  1.29 us (3%)
  other arithmetic  0.72 us (2%)
    pallas_call x1, Pallas kernels, on_device(): pl.pallas_call(kernel, name='hyena_step', out_shape=[jax.ShapeDtypeStruct...  34 us
    unnamed x3, local copies, waits for them, and re-layouts  2.53 us

profile of v5, /device:TPU:1, one launch (start us, length us, event | category | flops | bytes accessed | tf_op | source)
XLA Modules:
  0.0 38.5 jit_solution(831728527037411032)
XLA Ops:
  1.3 0.7 %pad_maximum_fusion.small_hbm = f32[3,8,128]{2,1,0:T(8,128)S(1)} fusion(f32[1,8,128]{2,1,0:T(8,128)} %param.12, f32[1,8,128]{2,1,0:T(8,128)} %param.11, f32[1,8,128]{2,1,0:T(8,128)} %param.10), kind=kLoop, calls=%fused_computation | loop fusion | flops 6144 | bytes 24576 | tf_op jit(solution)/shard_map/concatenate | solution.py:513
  2.0 34.0 %hyena_step.1 = (bf16[1,128,4096]{2,1,0:T(8,128)(2,1)S(1)}, bf16[1,128,4096]{2,1,0:T(8,128)(2,1)S(1)}, f32[1,8,128]{2,1,0:T(8,128)S(1)}) custom-call(bf16[1,128,4096]{2,1,0:T(8,128)(2,1)} %x_hbm.1, bf16[1,128,4096]{2,1,0:T(8,128)(2,1)} %gate_hbm.1, bf16[1,128,4096]{2,1,0:T(8,128)(2,1)} %ct_hbm.1, f32[3,8,128]{2,1,0:T(8,128)S(1)} %pad_maximum_fusion.small_hbm, ...), custom_call_target="tpu_custom_call" | custom-call | flops 4294967296 | bytes 8388608 | tf_op jit(solution)/shard_map/hyena_step/pallas_call | solution.py:514
  36.0 1.0 %copy.14 = bf16[1,128,4096]{2,1,0:T(8,128)(2,1)} copy(bf16[1,128,4096]{2,1,0:T(8,128)(2,1)S(1)} %get-tuple-element.6) | data formatting | bytes 2097152
  36.9 1.0 %copy.15 = bf16[1,128,4096]{2,1,0:T(8,128)(2,1)} copy(bf16[1,128,4096]{2,1,0:T(8,128)(2,1)S(1)} %get-tuple-element.7) | data formatting | bytes 2097152
  37.9 0.6 %copy.16 = f32[1,8,128]{2,1,0:T(8,128)} copy(f32[1,8,128]{2,1,0:T(8,128)S(1)} %get-tuple-element.8) | data formatting | bytes 8192

commit v6 on v5

--- a/solution.py
+++ b/solution.py
@@ -445,7 +445,7 @@
     all_near().wait_recv()
     near_sum = jnp.sum(near[:, 0, :], axis=0, keepdims=True)
     far[0] = jnp.broadcast_to(near_sum, (8, 128))
-    for slot in range(1, 16):
+    for slot in reversed(range(1, 16)):
         to_far(slot, far.at[0, row], far.at[slot, row]).start()
     @pl.loop(HALF, CHUNKS - 2)
     def _(i):

time: 38.6 us -> 38.6 us (level)
  no operation moved by 1% of the time
where the time goes in v6:
time: 38.6 us; the launch traced here: 38.5 us
  Pallas kernels  34 us (88%)
  local copies, waits for them, and re-layouts  2.53 us (7%)
  between operations  1.29 us (3%)
  other arithmetic  0.72 us (2%)
    pallas_call x1, Pallas kernels, on_device(): pl.pallas_call(kernel, name='hyena_step', out_shape=[jax.ShapeDtypeStruct...  34 us
    unnamed x3, local copies, waits for them, and re-layouts  2.53 us

profile of v6, /device:TPU:1, one launch (start us, length us, event | category | flops | bytes accessed | tf_op | source)
XLA Modules:
  0.0 38.5 jit_solution(17943123848503515827)
XLA Ops:
  1.3 0.7 %pad_maximum_fusion.small_hbm = f32[3,8,128]{2,1,0:T(8,128)S(1)} fusion(f32[1,8,128]{2,1,0:T(8,128)} %param.12, f32[1,8,128]{2,1,0:T(8,128)} %param.11, f32[1,8,128]{2,1,0:T(8,128)} %param.10), kind=kLoop, calls=%fused_computation | loop fusion | flops 6144 | bytes 24576 | tf_op jit(solution)/shard_map/concatenate | solution.py:513
  2.0 34.0 %hyena_step.1 = (bf16[1,128,4096]{2,1,0:T(8,128)(2,1)S(1)}, bf16[1,128,4096]{2,1,0:T(8,128)(2,1)S(1)}, f32[1,8,128]{2,1,0:T(8,128)S(1)}) custom-call(bf16[1,128,4096]{2,1,0:T(8,128)(2,1)} %x_hbm.1, bf16[1,128,4096]{2,1,0:T(8,128)(2,1)} %gate_hbm.1, bf16[1,128,4096]{2,1,0:T(8,128)(2,1)} %ct_hbm.1, f32[3,8,128]{2,1,0:T(8,128)S(1)} %pad_maximum_fusion.small_hbm, ...), custom_call_target="tpu_custom_call" | custom-call | flops 4294967296 | bytes 8388608 | tf_op jit(solution)/shard_map/hyena_step/pallas_call | solution.py:514
  36.0 1.0 %copy.14 = bf16[1,128,4096]{2,1,0:T(8,128)(2,1)} copy(bf16[1,128,4096]{2,1,0:T(8,128)(2,1)S(1)} %get-tuple-element.6) | data formatting | bytes 2097152
  36.9 1.0 %copy.15 = bf16[1,128,4096]{2,1,0:T(8,128)(2,1)} copy(bf16[1,128,4096]{2,1,0:T(8,128)(2,1)S(1)} %get-tuple-element.7) | data formatting | bytes 2097152
  37.9 0.6 %copy.16 = f32[1,8,128]{2,1,0:T(8,128)} copy(f32[1,8,128]{2,1,0:T(8,128)S(1)} %get-tuple-element.8) | data formatting | bytes 8192
